TPU v7x, 32 devices: a whole 2x2x4 slice. The times are simulated.
32 devices in a mesh: dp: 8 (over z, y), section: 4 (over x, core).
Axes of the slice: x: 2, y: 2, z: 4, core: 2. Of those that a mesh axis runs over, the one named last changes fastest.
Arguments:
- tokens: bfloat16 [16384, 768], P('dp'), may hold values from -6 to 6
- cotangent: bfloat16 [16384, 768], P('dp'), may hold values from -6 to 6
- segment_ids: int32 [64, 256], P('dp'), may hold values from 0 to 7, never falling along the last dimension, each value on 1 to 128 neighbouring positions
- first_weight: bfloat16 [4, 768, 3072], P('section')
- down_weight: bfloat16 [4, 768, 3072], P('section'), may hold values from -0.109375 to 0.109375
- ln_gain: float32 [4, 768], P('section'), may hold values from 0.5 to 1.5
- ln_shift: float32 [4, 768], P('section'), may hold values from -3 to 3
Outputs:
- layer_output: bfloat16 [16384, 768], P(('dp', 'section'))
- input_grad: bfloat16 [16384, 768], P(('dp', 'section'))
- first_grad: float32 [4, 768, 3072], P('section', None, 'dp')
- down_grad: float32 [4, 768, 3072], P('section', None, 'dp')
- gain_grad: float32 [4, 768], P('section', 'dp')
- shift_grad: float32 [4, 768], P('section', 'dp')
Inputs may be any that keep to these rules, and one draw needn't show every extreme that they name: `segment_ids`: along each row of 256 positions the numbers never fall; rows with equal numbers in one packed sequence form one document.
All inputs are finite; a program needn't handle non-finite values.
Results may differ from a plain program's by a relative error of at most 0.022.
Values may be sent and summed in bfloat16 or wider, within the bound.
A program may use at most 192 MiB of HBM per device.

v0:
```python
from functools import partial

import jax
import jax.numpy as jnp
from jax import lax
from jax.sharding import PartitionSpec as P

HEADS = 12


NORM_EPSILON = 1e-12
MASKED_SCORE = -1e30


def shifted(block, axis, distance):
    devices = range(lax.axis_size(axis))
    route = [(i - distance, i) for i in devices if i - distance in devices]
    return lax.ppermute(block, axis, route)


def layer_norm(residual, gain_row, shift_row):
    row_mean = jnp.mean(residual, axis=-1, keepdims=True)
    centered = residual - row_mean
    spread = jnp.mean(centered * centered, axis=-1, keepdims=True)
    return centered * lax.rsqrt(spread + NORM_EPSILON) * gain_row + shift_row


def attend_core(inputs, weight, segment_rows):
    seq_count, seq_length = segment_rows.shape
    model_width = inputs.shape[1]
    head_width = model_width // HEADS
    score_scale = head_width ** (-0.5)
    projected = jnp.dot(
        inputs, weight[:, : 3 * model_width], preferred_element_type=jnp.float32
    ).astype(jnp.bfloat16)
    projected = projected.reshape(seq_count, seq_length, 3, HEADS, head_width)
    queries = projected[:, :, 0]
    key_rows = projected[:, :, 1]
    values = projected[:, :, 2]
    scores = (
        jnp.einsum("bqhd,bkhd->bhqk", queries, key_rows, preferred_element_type=jnp.float32)
        * score_scale
    )
    allowed = (segment_rows[:, :, None] == segment_rows[:, None, :])[:, None]
    scores = jnp.where(allowed, scores, MASKED_SCORE)
    row_max = jnp.max(scores, axis=-1, keepdims=True)
    log_total = row_max + jnp.log(jnp.sum(jnp.exp(scores - row_max), axis=-1, keepdims=True))
    softmax_probs = jnp.exp(scores - log_total)
    probs_low = softmax_probs.astype(jnp.bfloat16)
    context = jnp.einsum("bhqk,bkhd->bqhd", probs_low, values, preferred_element_type=jnp.float32)
    context = context.astype(jnp.bfloat16).reshape(inputs.shape[0], model_width)
    return (queries, key_rows, values, softmax_probs, probs_low, context, score_scale)


def on_device(tokens, cotangent, segment_ids, first_weight, down_weight, ln_gain, ln_shift):
    section_count = lax.axis_size("section")
    section_index = lax.axis_index("section")
    final_section = section_count - 1
    model_width = tokens.shape[1]
    token_blocks = tokens.reshape(section_count, -1, model_width)
    cotangent_blocks = cotangent.reshape(section_count, -1, model_width)
    segment_blocks = segment_ids.reshape(section_count, -1, segment_ids.shape[1])
    block_rows = token_blocks.shape[1]
    weight = first_weight[0]
    down_rows = down_weight[0]
    gain_row = ln_gain[0]
    shift_row = ln_shift[0]
    hidden_width = weight.shape[1]
    kind_pick = 1 + section_index % 2

    def spare_forward(source, segment_rows):
        return jnp.zeros((block_rows, model_width), jnp.float32)

    def attend_forward(source, segment_rows):
        context = attend_core(source, weight, segment_rows)[5]
        branch = jnp.dot(context, weight[:, 3 * model_width :], preferred_element_type=jnp.float32)
        return layer_norm(source.astype(jnp.float32) + branch, gain_row, shift_row)

    def feed_forward(source, segment_rows):
        pre_gelu = jnp.dot(source, weight, preferred_element_type=jnp.float32)
        hidden = jax.nn.gelu(pre_gelu, approximate=False).astype(jnp.bfloat16)
        branch = jnp.einsum("rf,df->rd", hidden, down_rows, preferred_element_type=jnp.float32)
        return layer_norm(source.astype(jnp.float32) + branch, gain_row, shift_row)

    def spare_backward(source, upstream, segment_rows):
        return (
            jnp.zeros((block_rows, model_width), jnp.float32),
            jnp.zeros((model_width, hidden_width), jnp.float32),
            jnp.zeros((model_width, hidden_width), jnp.float32),
            jnp.zeros((model_width,), jnp.float32),
            jnp.zeros((model_width,), jnp.float32),
        )

    def attend_backward(source, upstream, segment_rows):
        queries, key_rows, values, softmax_probs, probs_low, context, score_scale = attend_core(
            source, weight, segment_rows
        )
        out_proj = weight[:, 3 * model_width :]
        in_proj = weight[:, : 3 * model_width]
        branch = jnp.dot(context, out_proj, preferred_element_type=jnp.float32)
        residual = source.astype(jnp.float32) + branch
        norm_value, norm_pull = jax.vjp(layer_norm, residual, gain_row, shift_row)
        d_resid, d_gain, d_shift = norm_pull(upstream.astype(jnp.float32))
        d_branch = d_resid.astype(jnp.bfloat16)
        d_out_proj = jnp.einsum("rd,re->de", context, d_branch, preferred_element_type=jnp.float32)
        d_context = jnp.einsum("re,de->rd", d_branch, out_proj, preferred_element_type=jnp.float32)
        d_context = d_context.astype(jnp.bfloat16).reshape(queries.shape)
        d_probs = jnp.einsum(
            "bqhd,bkhd->bhqk", d_context, values, preferred_element_type=jnp.float32
        )
        d_values = jnp.einsum(
            "bhqk,bqhd->bkhd", probs_low, d_context, preferred_element_type=jnp.float32
        )
        d_scores = softmax_probs * (
            d_probs - jnp.sum(d_probs * softmax_probs, axis=-1, keepdims=True)
        )
        d_scores = d_scores.astype(jnp.bfloat16)
        d_queries = (
            jnp.einsum("bhqk,bkhd->bqhd", d_scores, key_rows, preferred_element_type=jnp.float32)
            * score_scale
        )
        d_keys = (
            jnp.einsum("bhqk,bqhd->bkhd", d_scores, queries, preferred_element_type=jnp.float32)
            * score_scale
        )
        d_projected = jnp.stack([d_queries, d_keys, d_values], axis=2).astype(jnp.bfloat16)
        d_projected = d_projected.reshape(block_rows, 3 * model_width)
        d_in_proj = jnp.einsum("rd,re->de", source, d_projected, preferred_element_type=jnp.float32)
        d_source = d_resid + jnp.einsum(
            "re,de->rd", d_projected, in_proj, preferred_element_type=jnp.float32
        )
        d_first = jnp.concatenate([d_in_proj, d_out_proj], axis=1)
        return (d_source, d_first, jnp.zeros_like(d_first), d_gain, d_shift)

    def feed_backward(source, upstream, segment_rows):
        pre_gelu = jnp.dot(source, weight, preferred_element_type=jnp.float32)
        gelu_value, gelu_pull = jax.vjp(partial(jax.nn.gelu, approximate=False), pre_gelu)
        hidden = gelu_value.astype(jnp.bfloat16)
        branch = jnp.einsum("rf,df->rd", hidden, down_rows, preferred_element_type=jnp.float32)
        residual = source.astype(jnp.float32) + branch
        norm_value, norm_pull = jax.vjp(layer_norm, residual, gain_row, shift_row)
        d_resid, d_gain, d_shift = norm_pull(upstream.astype(jnp.float32))
        d_branch = d_resid.astype(jnp.bfloat16)
        d_down = jnp.einsum("rd,rf->df", d_branch, hidden, preferred_element_type=jnp.float32)
        d_hidden = jnp.dot(d_branch, down_rows, preferred_element_type=jnp.float32)
        d_pre = gelu_pull(d_hidden)[0].astype(jnp.bfloat16)
        d_first = jnp.einsum("rd,rf->df", source, d_pre, preferred_element_type=jnp.float32)
        d_source = d_resid + jnp.einsum(
            "rf,df->rd", d_pre, weight, preferred_element_type=jnp.float32
        )
        return (d_source, d_first, d_down, d_gain, d_shift)

    def run_ticks(tick_total, forward_lag, backward_lag, state_carry):

        def one_tick(tick_index, state_carry):
            arriving, returning, saved_inputs, layer_rows, input_rows, gradient_sums = state_carry
            if forward_lag is not None:
                batch_index = tick_index - forward_lag
                active = (batch_index >= 0) & (batch_index < section_count)
                batch_index = jnp.clip(batch_index, 0, section_count - 1)
                fresh = lax.dynamic_index_in_dim(token_blocks, batch_index, 0, keepdims=False)
                source = jnp.where(section_index == 0, fresh, arriving)
                segment_rows = lax.dynamic_index_in_dim(
                    segment_blocks, batch_index, 0, keepdims=False
                )
                branch_pick = jnp.where(active, kind_pick, 0)
                produced = lax.switch(
                    branch_pick, [spare_forward, attend_forward, feed_forward], source, segment_rows
                )
                outgoing = produced.astype(jnp.bfloat16)
                previous = lax.dynamic_index_in_dim(saved_inputs, batch_index, 0, keepdims=False)
                saved_inputs = lax.dynamic_update_index_in_dim(
                    saved_inputs, jnp.where(active, source, previous), batch_index, 0
                )
                previous = lax.dynamic_index_in_dim(layer_rows, batch_index, 0, keepdims=False)
                keep_output = active & (section_index == final_section)
                layer_rows = lax.dynamic_update_index_in_dim(
                    layer_rows, jnp.where(keep_output, outgoing, previous), batch_index, 0
                )
                arriving = shifted(outgoing, "section", 1)
            if backward_lag is not None:
                batch_index = tick_index - backward_lag
                active = (batch_index >= 0) & (batch_index < section_count)
                batch_index = jnp.clip(batch_index, 0, section_count - 1)
                fresh = lax.dynamic_index_in_dim(cotangent_blocks, batch_index, 0, keepdims=False)
                upstream = jnp.where(section_index == final_section, fresh, returning)
                source = lax.dynamic_index_in_dim(saved_inputs, batch_index, 0, keepdims=False)
                segment_rows = lax.dynamic_index_in_dim(
                    segment_blocks, batch_index, 0, keepdims=False
                )
                branch_pick = jnp.where(active, kind_pick, 0)
                results = lax.switch(
                    branch_pick,
                    [spare_backward, attend_backward, feed_backward],
                    source,
                    upstream,
                    segment_rows,
                )
                gradient_sums = tuple(
                    (running + addend for running, addend in zip(gradient_sums, results[1:]))
                )
                outgoing = results[0].astype(jnp.bfloat16)
                previous = lax.dynamic_index_in_dim(input_rows, batch_index, 0, keepdims=False)
                keep_grad = active & (section_index == 0)
                input_rows = lax.dynamic_update_index_in_dim(
                    input_rows, jnp.where(keep_grad, outgoing, previous), batch_index, 0
                )
                returning = shifted(outgoing, "section", -1)
            return (arriving, returning, saved_inputs, layer_rows, input_rows, gradient_sums)

        return lax.fori_loop(0, tick_total, one_tick, state_carry)

    row_zeros = jnp.zeros((block_rows, model_width), jnp.bfloat16)
    block_zeros = jnp.zeros((section_count, block_rows, model_width), jnp.bfloat16)
    starting_sums = (
        jnp.zeros((model_width, hidden_width), jnp.float32),
        jnp.zeros((model_width, hidden_width), jnp.float32),
        jnp.zeros((model_width,), jnp.float32),
        jnp.zeros((model_width,), jnp.float32),
    )
    state_carry = (row_zeros, row_zeros, block_zeros, block_zeros, block_zeros, starting_sums)
    state_carry = run_ticks(section_count + section_count - 1, section_index, None, state_carry)
    state_carry = run_ticks(
        section_count + section_count - 1, None, final_section - section_index, state_carry
    )
    layer_rows = state_carry[3]
    input_rows = state_carry[4]
    gradient_sums = state_carry[5]
    out_term = jnp.where(
        section_index == final_section, layer_rows.astype(jnp.float32), 0.0
    ).reshape(-1, model_width)
    grad_term = jnp.where(section_index == 0, input_rows.astype(jnp.float32), 0.0).reshape(
        -1, model_width
    )
    layer_sum, input_sum = (
        lax.psum_scatter(
            out_term.astype(jnp.bfloat16), "section", scatter_dimension=0, tiled=True
        ).astype(jnp.float32),
        lax.psum_scatter(
            grad_term.astype(jnp.bfloat16), "section", scatter_dimension=0, tiled=True
        ).astype(jnp.float32),
    )
    first_sum, down_sum, gain_sum, shift_sum = (
        lax.psum_scatter(gradient_sums[0][None], "dp", scatter_dimension=2, tiled=True),
        lax.psum_scatter(gradient_sums[1][None], "dp", scatter_dimension=2, tiled=True),
        lax.psum_scatter(gradient_sums[2][None, None], "dp", scatter_dimension=2, tiled=True),
        lax.psum_scatter(gradient_sums[3][None, None], "dp", scatter_dimension=2, tiled=True),
    )
    return (
        layer_sum.astype(jnp.bfloat16),
        input_sum.astype(jnp.bfloat16),
        first_sum,
        down_sum,
        gain_sum.reshape(1, -1),
        shift_sum.reshape(1, -1),
    )


def solution(mesh):
    return jax.shard_map(
        on_device,
        mesh=mesh,
        in_specs=(
            P("dp", None),
            P("dp", None),
            P("dp", None),
            P("section", None, None),
            P("section", None, None),
            P("section", None),
            P("section", None),
        ),
        out_specs=(
            P(("dp", "section"), None),
            P(("dp", "section"), None),
            P("section", None, "dp"),
            P("section", None, "dp"),
            P("section", "dp"),
            P("section", "dp"),
        ),
        check_vma=False,
    )
```

profile of v0, /device:TPU:1, one launch (start us, length us, event | category | flops | bytes accessed | tf_op | source)
XLA Modules:
  0.0 1500.9 jit_solution(1039326800206823837)
XLA Ops:
  11.9 237.1 %while.44 = (s32[]{:T(128)}, bf16[512,768]{1,0:T(8,128)(2,1)S(1)}, bf16[4,512,768]{2,1,0:T(8,128)(2,1)}, bf16[4,512,768]{2,1,0:T(8,128)(2,1)}, s32[]{:T(128)}, /...) while((s32[]{:T(128)}, bf16[512,768]{1,0:T(8,128)(2,1)S(1)}, ...), condition=%wide.region_10.11_spmd, body=%wide.region_0.10_spmd.sunk | while | flops 4939579904 | bytes 70733760 | solution.py:211
  44.2 21.6 %conditional.5 = (bf16[512,768]{1,0:T(8,128)(2,1)S(1)}) conditional(s32[]{:T(128)} %clamp.20, () %tuple.136, (bf16[512,768]{1,0:T(8,128)(2,1)}, bf16[768,3072]{1,0:T(8,128)(2,1)}, s32[4,2,256]{2,1,0:T(2,128)S(1)}, s32[]{:T(128)}, f32[1,768]{1,0:T(1,128)S(1)}, /*index=5*/f32[1,768]{1,0:T(1,128)S(1)}) %tuple.137, ...), branch_computations={%region_1.1_spmd, %region_2.6_spmd, %region_7.9_spmd} | conditional | flops 4938400256 | bytes 58148912 | solution.py:167
  44.2 20.9 %fusion.104 = (f32[512]{0:T(512)S(1)}, f32[512,768]{1,0:T(8,128)S(1)}) fusion(bf16[768,3072]{1,0:T(8,128)(2,1)} %get-tuple-element.678, bf16[512,768]{1,0:T(8,128)(2,1)} %get-tuple-element.676, bf16[768,3072]{1,0:T(8,128)(2,1)} %get-tuple-element.677), kind=kOutput, calls=%fused_computation.199 | convolution fusion | flops 4935253504 | bytes 11798528 | tf_op jit(solution)/shard_map/while/body/eval_jaxpr/cond/branch_2_fun/rf,df->rd/dot_general | solution.py:82
  80.6 21.6 %conditional.5 = (bf16[512,768]{1,0:T(8,128)(2,1)S(1)}) conditional(s32[]{:T(128)} %clamp.20, () %tuple.136, (bf16[512,768]{1,0:T(8,128)(2,1)}, bf16[768,3072]{1,0:T(8,128)(2,1)}, s32[4,2,256]{2,1,0:T(2,128)S(1)}, s32[]{:T(128)}, f32[1,768]{1,0:T(1,128)S(1)}, /*index=5*/f32[1,768]{1,0:T(1,128)S(1)}) %tuple.137, ...), branch_computations={%region_1.1_spmd, %region_2.6_spmd, %region_7.9_spmd} | conditional | flops 4938400256 | bytes 58148912 | solution.py:167
  80.6 20.9 %fusion.104 = (f32[512]{0:T(512)S(1)}, f32[512,768]{1,0:T(8,128)S(1)}) fusion(bf16[768,3072]{1,0:T(8,128)(2,1)} %get-tuple-element.678, bf16[512,768]{1,0:T(8,128)(2,1)} %get-tuple-element.676, bf16[768,3072]{1,0:T(8,128)(2,1)} %get-tuple-element.677), kind=kOutput, calls=%fused_computation.199 | convolution fusion | flops 4935253504 | bytes 11798528 | tf_op jit(solution)/shard_map/while/body/eval_jaxpr/cond/branch_2_fun/rf,df->rd/dot_general | solution.py:82
  119.3 21.6 %conditional.5 = (bf16[512,768]{1,0:T(8,128)(2,1)S(1)}) conditional(s32[]{:T(128)} %clamp.20, () %tuple.136, (bf16[512,768]{1,0:T(8,128)(2,1)}, bf16[768,3072]{1,0:T(8,128)(2,1)}, s32[4,2,256]{2,1,0:T(2,128)S(1)}, s32[]{:T(128)}, f32[1,768]{1,0:T(1,128)S(1)}, /*index=5*/f32[1,768]{1,0:T(1,128)S(1)}) %tuple.137, ...), branch_computations={%region_1.1_spmd, %region_2.6_spmd, %region_7.9_spmd} | conditional | flops 4938400256 | bytes 58148912 | solution.py:167
  158.1 21.6 %conditional.5 = (bf16[512,768]{1,0:T(8,128)(2,1)S(1)}) conditional(s32[]{:T(128)} %clamp.20, () %tuple.136, (bf16[512,768]{1,0:T(8,128)(2,1)}, bf16[768,3072]{1,0:T(8,128)(2,1)}, s32[4,2,256]{2,1,0:T(2,128)S(1)}, s32[]{:T(128)}, f32[1,768]{1,0:T(1,128)S(1)}, /*index=5*/f32[1,768]{1,0:T(1,128)S(1)}) %tuple.137, ...), branch_computations={%region_1.1_spmd, %region_2.6_spmd, %region_7.9_spmd} | conditional | flops 4938400256 | bytes 58148912 | solution.py:167
  196.9 25.9 %collective-permute-start = (bf16[512,768]{1,0:T(8,128)(2,1)S(1)}, bf16[512,768]{1,0:T(8,128)(2,1)S(1)}, u32[]{:S(2)}, u32[]{:S(2)}) collective-permute-start(bf16[512,768]{1,0:T(8,128)(2,1)S(1)} %get-tuple-element.1267), channel_id=1, source_target_pairs={{0,1},{1,2},{2,3},{4,5},{5,6},{6,7},{8,9},{9,10},{10,11},{12,13},{... | collective-permute-start | bytes 2359304 | tf_op jit(solution)/shard_map/while/body/eval_jaxpr/ppermute | solution.py:18
  250.9 697.6 %while.45 = (s32[]{:T(128)}, bf16[512,768]{1,0:T(8,128)(2,1)S(1)}, bf16[4,512,768]{2,1,0:T(8,128)(2,1)}, f32[768,3072]{0,1:T(8,128)}, f32[768,3072]{1,0:T(8,128)...) while((s32[]{:T(128)}, bf16[512,768]{1,0:T(8,128)(2,1)S(1)}, ...), condition=%wide.region_31.32_spmd.clone, body=%wide.region_12.31_spmd.clone.sunk | while | flops 14641796096 | bytes 337944064 | solution.py:211
  331.7 89.9 %collective-permute-done.1 = bf16[512,768]{1,0:T(8,128)(2,1)S(1)} collective-permute-done((bf16[512,768]{1,0:T(8,128)(2,1)}, bf16[512,768]{1,0:T(8,128)(2,1)S(1)}, u32[]{:S(2)}, u32[]{:S(2)}) %collective-permute-start.1) | collective-permute-done | bytes 786464 | tf_op jit(solution)/shard_map/while/body/eval_jaxpr/ppermute | solution.py:18
  424.1 56.0 %conditional.6 = (f32[768,3072]{0,1:T(8,128)}, f32[768,3072]{1,0:T(8,128)}, f32[768]{0:T(1024)S(1)}, f32[768]{0:T(1024)S(1)}, bf16[512,768]{1,0:T(8,128)(2,1)}) conditional(s32[]{:T(128)} %clamp.21, () %tuple.141, (bf16[768,3072]{1,0:T(8,128)(2,1)}, bf16[512,768]{1,0:T(8,128)(2,1)S(1)}, s32[4,2,256]{2,1,0:T(2,128)S(1)}, ...), branch_computations={%region_13.13_spmd, %region_14.23_spmd, %region_24.30_spmd} | conditional | flops 14631569408 | bytes 270242272 | solution.py:192
  508.8 27.8 %collective-permute-done.1 = bf16[512,768]{1,0:T(8,128)(2,1)S(1)} collective-permute-done((bf16[512,768]{1,0:T(8,128)(2,1)}, bf16[512,768]{1,0:T(8,128)(2,1)S(1)}, u32[]{:S(2)}, u32[]{:S(2)}) %collective-permute-start.1) | collective-permute-done | bytes 786464 | tf_op jit(solution)/shard_map/while/body/eval_jaxpr/ppermute | solution.py:18
  539.1 47.9 %conditional.6 = (f32[768,3072]{0,1:T(8,128)}, f32[768,3072]{1,0:T(8,128)}, f32[768]{0:T(1024)S(1)}, f32[768]{0:T(1024)S(1)}, bf16[512,768]{1,0:T(8,128)(2,1)}) conditional(s32[]{:T(128)} %clamp.21, () %tuple.141, (bf16[768,3072]{1,0:T(8,128)(2,1)}, bf16[512,768]{1,0:T(8,128)(2,1)S(1)}, s32[4,2,256]{2,1,0:T(2,128)S(1)}, ...), branch_computations={%region_13.13_spmd, %region_14.23_spmd, %region_24.30_spmd} | conditional | flops 14631569408 | bytes 270242272 | solution.py:192
  615.8 35.5 %collective-permute-done.1 = bf16[512,768]{1,0:T(8,128)(2,1)S(1)} collective-permute-done((bf16[512,768]{1,0:T(8,128)(2,1)}, bf16[512,768]{1,0:T(8,128)(2,1)S(1)}, u32[]{:S(2)}, u32[]{:S(2)}) %collective-permute-start.1) | collective-permute-done | bytes 786464 | tf_op jit(solution)/shard_map/while/body/eval_jaxpr/ppermute | solution.py:18
  653.7 47.9 %conditional.6 = (f32[768,3072]{0,1:T(8,128)}, f32[768,3072]{1,0:T(8,128)}, f32[768]{0:T(1024)S(1)}, f32[768]{0:T(1024)S(1)}, bf16[512,768]{1,0:T(8,128)(2,1)}) conditional(s32[]{:T(128)} %clamp.21, () %tuple.141, (bf16[768,3072]{1,0:T(8,128)(2,1)}, bf16[512,768]{1,0:T(8,128)(2,1)S(1)}, s32[4,2,256]{2,1,0:T(2,128)S(1)}, ...), branch_computations={%region_13.13_spmd, %region_14.23_spmd, %region_24.30_spmd} | conditional | flops 14631569408 | bytes 270242272 | solution.py:192
  730.3 35.9 %collective-permute-done.1 = bf16[512,768]{1,0:T(8,128)(2,1)S(1)} collective-permute-done((bf16[512,768]{1,0:T(8,128)(2,1)}, bf16[512,768]{1,0:T(8,128)(2,1)S(1)}, u32[]{:S(2)}, u32[]{:S(2)}) %collective-permute-start.1) | collective-permute-done | bytes 786464 | tf_op jit(solution)/shard_map/while/body/eval_jaxpr/ppermute | solution.py:18
  768.6 47.9 %conditional.6 = (f32[768,3072]{0,1:T(8,128)}, f32[768,3072]{1,0:T(8,128)}, f32[768]{0:T(1024)S(1)}, f32[768]{0:T(1024)S(1)}, bf16[512,768]{1,0:T(8,128)(2,1)}) conditional(s32[]{:T(128)} %clamp.21, () %tuple.141, (bf16[768,3072]{1,0:T(8,128)(2,1)}, bf16[512,768]{1,0:T(8,128)(2,1)S(1)}, s32[4,2,256]{2,1,0:T(2,128)S(1)}, ...), branch_computations={%region_13.13_spmd, %region_14.23_spmd, %region_24.30_spmd} | conditional | flops 14631569408 | bytes 270242272 | solution.py:192
  858.0 59.8 %collective-permute-start.1 = (bf16[512,768]{1,0:T(8,128)(2,1)}, bf16[512,768]{1,0:T(8,128)(2,1)S(1)}, u32[]{:S(2)}, u32[]{:S(2)}) collective-permute-start(bf16[512,768]{1,0:T(8,128)(2,1)} %get-tuple-element.1122), channel_id=1, source_target_pairs={{1,0},{2,1},{3,2},{5,4},{6,5},{7,6},{9,8},{10,9},{11,10},{13,12},{... | collective-permute-start | bytes 2359304 | tf_op jit(solution)/shard_map/while/body/eval_jaxpr/ppermute | solution.py:18
  971.9 41.0 %reduce-scatter.19.cloned.1.call-done = f32[96,1]{1,0:T(8,128)} async-done(((f32[768,1]{1,0:T(8,128)}), f32[96,1]{1,0:T(8,128)}) %reduce-scatter.19.cloned.1.call-update) | async-done | bytes 400
  1014.2 62.4 %reduce-scatter.21.cloned.1.call-done = f32[96,1]{1,0:T(8,128)} async-done(((f32[768,1]{1,0:T(8,128)}), f32[96,1]{1,0:T(8,128)}) %reduce-scatter.21.cloned.1.call-update) | async-done | bytes 400
  1078.0 40.7 %reduce-scatter.11.cloned.1.call-done = bf16[512,768]{1,0:T(8,128)(2,1)} async-done(((bf16[2048,768]{1,0:T(8,128)(2,1)}), bf16[512,768]{1,0:T(8,128)(2,1)}) %reduce-scatter.11.cloned.1.call-update) | async-done | bytes 786448 | tf_op jit(solution)/shard_map/reduce_scatter | solution.py:236
  1118.6 41.1 %reduce-scatter.13.cloned.1.call-done = bf16[512,768]{1,0:T(8,128)(2,1)} async-done(((bf16[2048,768]{1,0:T(8,128)(2,1)}), bf16[512,768]{1,0:T(8,128)(2,1)}) %reduce-scatter.13.cloned.1.call-update) | async-done | bytes 786448 | tf_op jit(solution)/shard_map/reduce_scatter | solution.py:239
  1159.7 167.6 %reduce-scatter.15.cloned.1.call-done = f32[1,768,384]{2,1,0:T(8,128)} async-done(((f32[1,768,3072]{2,1,0:T(8,128)}), f32[1,768,384]{2,1,0:T(8,128)}) %reduce-scatter.15.cloned.1.call-update) | async-done | bytes 1179664 | tf_op jit(solution)/shard_map/reduce_scatter | solution.py:244
  1327.2 166.6 %reduce-scatter.17.cloned.1.call-done = f32[1,768,384]{2,1,0:T(8,128)} async-done(((f32[1,768,3072]{2,1,0:T(8,128)}), f32[1,768,384]{2,1,0:T(8,128)}) %reduce-scatter.17.cloned.1.call-update) | async-done | bytes 1179664 | tf_op jit(solution)/shard_map/reduce_scatter | solution.py:245
  (356 shorter events, 666.6 us)
Async XLA Ops:
  7.2 1005.6 %reduce-scatter.19.cloned.1.call-start = ((), (), s32[]{:S(2)}) async-start(), calls=%async_computation.10 | async-start | bytes 442368
  15.8 24.6 %collective-permute-start = (bf16[512,768]{1,0:T(8,128)(2,1)S(1)}, bf16[512,768]{1,0:T(8,128)(2,1)S(1)}, u32[]{:S(2)}, u32[]{:S(2)}) collective-permute-start(bf16[512,768]{1,0:T(8,128)(2,1)S(1)} %get-tuple-element.1267), channel_id=1, source_target_pairs={{0,1},{1,2},{2,3},{4,5},{5,6},{6,7},{8,9},{9,10},{10,11},{12,13},{... | collective-permute-start | bytes 2359304 | tf_op jit(solution)/shard_map/while/body/eval_jaxpr/ppermute | solution.py:18
  65.9 10.8 collective-permute-start
  102.2 13.2 collective-permute-start
  140.9 13.3 collective-permute-start
  179.7 13.2 collective-permute-start
  196.9 34.8 %collective-permute-start = (bf16[512,768]{1,0:T(8,128)(2,1)S(1)}, bf16[512,768]{1,0:T(8,128)(2,1)S(1)}, u32[]{:S(2)}, u32[]{:S(2)}) collective-permute-start(bf16[512,768]{1,0:T(8,128)(2,1)S(1)} %get-tuple-element.1267), channel_id=1, source_target_pairs={{0,1},{1,2},{2,3},{4,5},{5,6},{6,7},{8,9},{9,10},{10,11},{12,13},{... | collective-permute-start | bytes 2359304 | tf_op jit(solution)/shard_map/while/body/eval_jaxpr/ppermute | solution.py:18
  235.7 13.3 collective-permute-start
  267.0 23.2 %collective-permute-start.1 = (bf16[512,768]{1,0:T(8,128)(2,1)}, bf16[512,768]{1,0:T(8,128)(2,1)S(1)}, u32[]{:S(2)}, u32[]{:S(2)}) collective-permute-start(bf16[512,768]{1,0:T(8,128)(2,1)} %get-tuple-element.1122), channel_id=1, source_target_pairs={{1,0},{2,1},{3,2},{5,4},{6,5},{7,6},{9,8},{10,9},{11,10},{13,12},{... | collective-permute-start | bytes 2359304 | tf_op jit(solution)/shard_map/while/body/eval_jaxpr/ppermute | solution.py:18
  302.9 118.7 %collective-permute-start.1 = (bf16[512,768]{1,0:T(8,128)(2,1)}, bf16[512,768]{1,0:T(8,128)(2,1)S(1)}, u32[]{:S(2)}, u32[]{:S(2)}) collective-permute-start(bf16[512,768]{1,0:T(8,128)(2,1)} %get-tuple-element.1122), channel_id=1, source_target_pairs={{1,0},{2,1},{3,2},{5,4},{6,5},{7,6},{9,8},{10,9},{11,10},{13,12},{... | collective-permute-start | bytes 2359304 | tf_op jit(solution)/shard_map/while/body/eval_jaxpr/ppermute | solution.py:18
  330.6 91.0 %copy-start.22 = (f32[768]{0:T(1024)}, f32[768]{0:T(1024)S(1)}, u32[]{:S(2)}) copy-start(f32[768]{0:T(1024)S(1)} %get-tuple-element.1250) | copy-start | bytes 9220 | tf_op jit(solution)/shard_map/while
  330.6 91.0 %copy-start.24 = (f32[768]{0:T(1024)}, f32[768]{0:T(1024)S(1)}, u32[]{:S(2)}) copy-start(f32[768]{0:T(1024)S(1)} %get-tuple-element.1251) | copy-start | bytes 9220 | tf_op jit(solution)/shard_map/while
  480.0 56.6 %collective-permute-start.1 = (bf16[512,768]{1,0:T(8,128)(2,1)}, bf16[512,768]{1,0:T(8,128)(2,1)S(1)}, u32[]{:S(2)}, u32[]{:S(2)}) collective-permute-start(bf16[512,768]{1,0:T(8,128)(2,1)} %get-tuple-element.1122), channel_id=1, source_target_pairs={{1,0},{2,1},{3,2},{5,4},{6,5},{7,6},{9,8},{10,9},{11,10},{13,12},{... | collective-permute-start | bytes 2359304 | tf_op jit(solution)/shard_map/while/body/eval_jaxpr/ppermute | solution.py:18
  587.0 64.2 %collective-permute-start.1 = (bf16[512,768]{1,0:T(8,128)(2,1)}, bf16[512,768]{1,0:T(8,128)(2,1)S(1)}, u32[]{:S(2)}, u32[]{:S(2)}) collective-permute-start(bf16[512,768]{1,0:T(8,128)(2,1)} %get-tuple-element.1122), channel_id=1, source_target_pairs={{1,0},{2,1},{3,2},{5,4},{6,5},{7,6},{9,8},{10,9},{11,10},{13,12},{... | collective-permute-start | bytes 2359304 | tf_op jit(solution)/shard_map/while/body/eval_jaxpr/ppermute | solution.py:18
  701.6 64.6 %collective-permute-start.1 = (bf16[512,768]{1,0:T(8,128)(2,1)}, bf16[512,768]{1,0:T(8,128)(2,1)S(1)}, u32[]{:S(2)}, u32[]{:S(2)}) collective-permute-start(bf16[512,768]{1,0:T(8,128)(2,1)} %get-tuple-element.1122), channel_id=1, source_target_pairs={{1,0},{2,1},{3,2},{5,4},{6,5},{7,6},{9,8},{10,9},{11,10},{13,12},{... | collective-permute-start | bytes 2359304 | tf_op jit(solution)/shard_map/while/body/eval_jaxpr/ppermute | solution.py:18
  729.3 37.0 %copy-start.22 = (f32[768]{0:T(1024)}, f32[768]{0:T(1024)S(1)}, u32[]{:S(2)}) copy-start(f32[768]{0:T(1024)S(1)} %get-tuple-element.1250) | copy-start | bytes 9220 | tf_op jit(solution)/shard_map/while
  729.3 36.9 %copy-start.24 = (f32[768]{0:T(1024)}, f32[768]{0:T(1024)S(1)}, u32[]{:S(2)}) copy-start(f32[768]{0:T(1024)S(1)} %get-tuple-element.1251) | copy-start | bytes 9220 | tf_op jit(solution)/shard_map/while
  816.5 28.8 %collective-permute-start.1 = (bf16[512,768]{1,0:T(8,128)(2,1)}, bf16[512,768]{1,0:T(8,128)(2,1)S(1)}, u32[]{:S(2)}, u32[]{:S(2)}) collective-permute-start(bf16[512,768]{1,0:T(8,128)(2,1)} %get-tuple-element.1122), channel_id=1, source_target_pairs={{1,0},{2,1},{3,2},{5,4},{6,5},{7,6},{9,8},{10,9},{11,10},{13,12},{... | collective-permute-start | bytes 2359304 | tf_op jit(solution)/shard_map/while/body/eval_jaxpr/ppermute | solution.py:18
  858.0 86.7 %collective-permute-start.1 = (bf16[512,768]{1,0:T(8,128)(2,1)}, bf16[512,768]{1,0:T(8,128)(2,1)S(1)}, u32[]{:S(2)}, u32[]{:S(2)}) collective-permute-start(bf16[512,768]{1,0:T(8,128)(2,1)} %get-tuple-element.1122), channel_id=1, source_target_pairs={{1,0},{2,1},{3,2},{5,4},{6,5},{7,6},{9,8},{10,9},{11,10},{13,12},{... | collective-permute-start | bytes 2359304 | tf_op jit(solution)/shard_map/while/body/eval_jaxpr/ppermute | solution.py:18
  951.8 124.8 %reduce-scatter.21.cloned.1.call-start = ((), (), s32[]{:S(2)}) async-start(), calls=%async_computation.11 | async-start | bytes 442368
  955.0 163.6 %reduce-scatter.11.cloned.1.call-start = ((), (), s32[]{:S(2)}) async-start(), calls=%async_computation.6 | async-start | bytes 3932160 | tf_op jit(solution)/shard_map/reduce_scatter | solution.py:236
  959.2 200.5 %reduce-scatter.13.cloned.1.call-start = ((), (), s32[]{:S(2)}) async-start(), calls=%async_computation.7 | async-start | bytes 3932160 | tf_op jit(solution)/shard_map/reduce_scatter | solution.py:239
  961.5 365.7 %reduce-scatter.15.cloned.1.call-start = ((), (), s32[]{:S(2)}) async-start(), calls=%async_computation.8 | async-start | bytes 10616832 | tf_op jit(solution)/shard_map/reduce_scatter | solution.py:244
  971.3 522.5 %reduce-scatter.17.cloned.1.call-start = ((), (), s32[]{:S(2)}) async-start(), calls=%async_computation.9 | async-start | bytes 10616832 | tf_op jit(solution)/shard_map/reduce_scatter | solution.py:245
  (55 other events, 639.5 us)
Sparse Core Ops, SparseCore 0:
  951.9 60.8 reduce-scatter.18
  1016.1 60.4 reduce-scatter.20
  1079.7 38.8 reduce-scatter.10
  1121.7 37.9 reduce-scatter.12
  1163.7 163.5 reduce-scatter.14
  1331.3 162.5 reduce-scatter.16
where the time goes:
time: 1530 us; the launch traced here: 1500 us
  waiting for transfers between devices  767 us (50%)
  matrix products  267 us (17%)
  other arithmetic  224 us (15%)
  starting transfers between devices  121 us (8%)
  local copies, waits for them, and re-layouts  89.2 us (6%)
  loops' own time  17.9 us (1%)
    ppermute x14, waiting for transfers between devices, shifted(): return lax.ppermute(block, axis, route)  247 us
    reduce_scatter x1, waiting for transfers between devices, on_device(): lax.psum_scatter(gradient_sums[0][None], 'dp', scatter_dimension=2, tiled...  168 us
    reduce_scatter x1, waiting for transfers between devices, on_device(): lax.psum_scatter(gradient_sums[1][None], 'dp', scatter_dimension=2, tiled...  167 us
    add x21, other arithmetic, one_tick(): running + addend  166 us
    ppermute x14, starting transfers between devices, shifted(): return lax.ppermute(block, axis, route)  121 us
    unnamed x8, waiting for transfers between devices  104 us
    dot_general x4, matrix products, feed_forward(): jnp.einsum('rf,df->rd', hidden, down_rows, preferred_element_type=jnp.flo...  83.8 us
    dot_general x4, matrix products, feed_backward(): pre_gelu = jnp.dot(source, weight, preferred_element_type=jnp.float32)  74.5 us
  transfers between devices with their start and end apart: 20, of which 17 were waited for; matrix products, arithmetic and copies ran while one was open for 15% of the time, Pallas kernels for 0%

commit v1 on v0

v1 whole, which is shorter than its diff:
```python
import functools

import jax
import jax.numpy as jnp
from jax import lax
from jax.experimental import pallas as pl
from jax.experimental.pallas import tpu as pltpu
from jax.sharding import PartitionSpec as P

HEADS = 12
NORM_EPSILON = 1e-12
MASKED_SCORE = -1e30
INV_SQRT2 = 0.7071067811865476
INV_SQRT2PI = 0.3989422804014327
MESH = pl.DeviceIdType.MESH
bf16 = jnp.bfloat16
f32 = jnp.float32


def dot(a, b):
    return jnp.dot(a, b, preferred_element_type=f32)


def dot_nt(a, b):
    return lax.dot_general(a, b, (((1,), (1,)), ((), ())), preferred_element_type=f32)


def dot_tn(a, b):
    return lax.dot_general(a, b, (((0,), (0,)), ((), ())), preferred_element_type=f32)


def aligned(index, size):
    return pl.ds(pl.multiple_of(index * size, size), size)


def norm_forward(residual, rows, gain, shift, refs):
    mean = jnp.mean(residual, axis=-1, keepdims=True)
    centered = residual - mean
    spread = jnp.mean(centered * centered, axis=-1, keepdims=True)
    scale = lax.rsqrt(spread + NORM_EPSILON)
    normal = centered * scale
    refs.normal[rows, :] = normal.astype(bf16)
    refs.scale[rows, :] = scale
    refs.out[rows, :] = (normal * gain + shift).astype(bf16)


def norm_backward(rows, gain, refs):
    upstream = refs.grad[rows, :].astype(f32)
    normal = refs.normal[rows, :].astype(f32)
    scale = refs.scale[rows, :]
    count, width = upstream.shape
    refs.norm_sums[0] += jnp.sum((upstream * normal).reshape(count // 8, 8, width), axis=0)
    refs.norm_sums[1] += jnp.sum(upstream.reshape(count // 8, 8, width), axis=0)
    pulled = upstream * gain
    mean = jnp.mean(pulled, axis=-1, keepdims=True)
    along = jnp.mean(pulled * normal, axis=-1, keepdims=True)
    d_resid = scale * (pulled - mean - normal * along)
    refs.grad[rows, :] = d_resid.astype(bf16)
    return d_resid


def feed_forward(rows, gain, shift, refs):
    width, hidden = refs.weight.shape
    tile = width
    tiles = hidden // tile
    source = refs.rows_in[rows, :]
    residual = source.astype(f32)

    def up(t):
        return dot(source, refs.weight[:, t * tile : (t + 1) * tile])

    def down(value, t):
        return dot_nt(value, refs.down[:, t * tile : (t + 1) * tile])

    pre = up(0)
    held = None
    for t in range(tiles):
        following = up(t + 1) if t + 1 < tiles else None
        cdf = 0.5 + 0.5 * lax.erf(pre * INV_SQRT2)
        value = (pre * cdf).astype(bf16)
        slope = cdf + pre * (INV_SQRT2PI * jnp.exp(-0.5 * pre * pre))
        refs.keep[rows, t * tile : (t + 1) * tile] = value
        refs.wide[rows, t * tile : (t + 1) * tile] = slope.astype(bf16)
        if held is not None:
            residual = residual + down(held, t - 1)
        held, pre = value, following
    residual = residual + down(held, tiles - 1)
    norm_forward(residual, rows, gain, shift, refs)


def feed_backward(rows, gain, refs):
    width, hidden = refs.weight.shape
    tile = width
    tiles = hidden // tile
    d_resid = norm_backward(rows, gain, refs)
    d_branch = d_resid.astype(bf16)
    total = d_resid

    def up(t):
        return dot(d_branch, refs.down[:, t * tile : (t + 1) * tile])

    def down(value, t):
        return dot_nt(value, refs.weight[:, t * tile : (t + 1) * tile])

    d_hidden = up(0)
    held = None
    for t in range(tiles):
        following = up(t + 1) if t + 1 < tiles else None
        columns = slice(t * tile, (t + 1) * tile)
        d_pre = (d_hidden * refs.wide[rows, columns].astype(f32)).astype(bf16)
        refs.wide[rows, columns] = d_pre
        if held is not None:
            total = total + down(held, t - 1)
        held, d_hidden = d_pre, following
    total = total + down(held, tiles - 1)
    refs.d_in[rows, :] = total.astype(bf16)


def head_part(refs, first_row, length, blocks, which, n):
    head_width = refs.weight.shape[0] // HEADS
    per_block = length // head_width
    column = (which * blocks + n // per_block) * length
    rows = pl.ds(pl.multiple_of(first_row + (n % per_block) * head_width, head_width), head_width)
    return rows, slice(column, column + length)


def attend_forward(index, gain, shift, refs):
    length = refs.segments.shape[1]
    width = refs.weight.shape[0]
    blocks = width // length
    rows = aligned(index, length)
    first_row = index * length
    source = refs.rows_in[rows, :]
    ids = jnp.broadcast_to(refs.segments[pl.ds(index, 1), :].astype(f32), (length, length))
    allowed = ids == ids.T
    score_scale = (width // HEADS) ** (-0.5)
    for which in range(3):
        turned = dot_nt(refs.down[:, which * width : (which + 1) * width], source)
        if which == 0:
            turned = turned * score_scale
        turned = turned.astype(bf16)
        for j in range(blocks):
            column = (which * blocks + j) * length
            refs.keep[rows, column : column + length] = turned[j * length : (j + 1) * length, :]
    place = functools.partial(head_part, refs, first_row, length, blocks)

    def score(n):
        return dot_tn(refs.keep[place(1, n)], refs.keep[place(0, n)])

    def weigh(scores):
        scores = jnp.where(allowed, scores, MASKED_SCORE)
        raw = jnp.exp(scores - jnp.max(scores, axis=0, keepdims=True))
        return raw.astype(bf16), 1.0 / jnp.sum(raw, axis=0, keepdims=True)

    def finish(n, raw, inverse):
        refs.wide[rows, n * length : (n + 1) * length] = raw
        refs.inverse[pl.ds(index * 16 + n, 1), :] = inverse
        refs.keep[place(3, n)] = (dot(refs.keep[place(2, n)], raw) * inverse).astype(bf16)

    ahead = 2
    scores = [score(n) for n in range(ahead)]
    held = None
    for n in range(HEADS):
        if n + ahead < HEADS:
            scores.append(score(n + ahead))
        current = weigh(scores[n])
        if held is not None:
            finish(n - 1, *held)
        held = current
    finish(HEADS - 1, *held)
    residual = source.astype(f32)
    for j in range(blocks):
        column = (3 * blocks + j) * length
        residual = residual + dot_tn(
            refs.keep[rows, column : column + length],
            refs.weight[j * length : (j + 1) * length, 3 * width :],
        )
    norm_forward(residual, rows, gain, shift, refs)


def attend_backward(index, gain, refs):
    length = refs.segments.shape[1]
    width = refs.weight.shape[0]
    head_width = width // HEADS
    blocks = width // length
    per_block = length // head_width
    score_scale = head_width ** (-0.5)
    rows = aligned(index, length)
    first_row = index * length
    d_resid = norm_backward(rows, gain, refs)
    refs.d_context[...] = dot_nt(refs.weight[:, 3 * width :], d_resid.astype(bf16))
    place = functools.partial(head_part, refs, first_row, length, blocks)

    def first(n):
        inverse = refs.inverse[pl.ds(index * 16 + n, 1), :]
        d_context = refs.d_context[n * head_width : (n + 1) * head_width, :] * inverse
        along = jnp.sum(d_context * refs.keep[place(3, n)].astype(f32), axis=0, keepdims=True)
        d_context = d_context.astype(bf16)
        return dot_tn(refs.keep[place(2, n)], d_context), along, d_context

    def second(n, d_probs, along, d_context):
        raw = refs.wide[rows, n * length : (n + 1) * length]
        return (raw.astype(f32) * (d_probs - along)).astype(bf16), raw, d_context

    made = ([], [], [])

    def third(n, d_scores, raw, d_context):
        made[0].append(dot(refs.keep[place(1, n)], d_scores) * score_scale)
        made[1].append(dot_nt(refs.keep[place(0, n)], d_scores))
        made[2].append(dot_nt(d_context, raw))
        if n % per_block == per_block - 1:
            block = n // per_block
            for which in range(3):
                column = (which * blocks + block) * length
                whole = jnp.concatenate(made[which], axis=0).astype(bf16)
                refs.keep[rows, column : column + length] = whole.T
                made[which].clear()
            column = (3 * blocks + block) * length
            refs.keep[rows, column : column + length] = refs.keep[rows, column : column + length].T

    current = first(0)
    held = None
    for n in range(HEADS):
        following = first(n + 1) if n + 1 < HEADS else None
        ready = second(n, *current)
        if held is not None:
            third(n - 1, *held)
        held, current = ready, following
    third(HEADS - 1, *held)
    d_in = d_resid + dot_nt(refs.keep[rows, : 3 * width], refs.weight[:, : 3 * width])
    refs.d_in[rows, :] = d_in.astype(bf16)


class Refs:
    def __init__(self, **named):
        self.__dict__.update(named)


def pipeline(
    sections,
    tokens,
    cotangent,
    segments,
    weight_in,
    down_in,
    gain_in,
    shift_in,
    layer_out,
    input_out,
    weight_sums,
    norm_out,
    rows_in,
    keep,
    wide,
    grad,
    normal,
    scale,
    out,
    d_in,
    weight,
    down,
    norm_sums,
    d_context,
    inverse,
    load_sem,
    first_sem,
    forward_send,
    forward_recv,
    backward_send,
    backward_recv,
    share_send,
    share_recv,
    store_sem,
):
    dp = lax.axis_index("dp")
    section = lax.axis_index("section")
    batches, length = segments.shape
    width, hidden = weight.shape
    share = batches // sections
    final = sections - 1
    refs = Refs(
        rows_in=rows_in, keep=keep, wide=wide, grad=grad, normal=normal, scale=scale, out=out, d_in=d_in,
        weight=weight, down=down, norm_sums=norm_sums, d_context=d_context, inverse=inverse, segments=segments,
    )
    is_attention = lax.rem(section, 2) == 0
    is_feed = lax.rem(section, 2) == 1

    def load_rows(source, target, i):
        rows = aligned(i, length)
        return pltpu.make_async_copy(source.at[rows, :], target.at[rows, :], first_sem.at[i])

    load_weight = pltpu.make_async_copy(weight_in.at[0], weight, load_sem.at[0])
    load_down = pltpu.make_async_copy(down_in.at[0], down, load_sem.at[1])
    load_weight.start()

    @pl.when(is_feed)
    def _():
        load_down.start()

    @pl.when(section == 0)
    def _():
        for i in range(batches):
            load_rows(tokens, rows_in, i).start()

    @pl.when(section == final)
    def _():
        for i in range(batches):
            load_rows(cotangent, grad, i).start()

    barrier = pltpu.get_barrier_semaphore()
    for other in range(1, sections):
        pl.semaphore_signal(
            barrier, inc=1, device_id=(dp, lax.rem(section + other, sections)), device_id_type=MESH
        )
    pl.semaphore_wait(barrier, sections - 1)

    norm_sums[...] = jnp.zeros_like(norm_sums)
    gain = gain_in[...]
    shift = shift_in[...]

    def forward_copy(i):
        rows = aligned(i, length)
        return pltpu.make_async_remote_copy(
            out.at[rows, :], rows_in.at[rows, :], forward_send.at[i], forward_recv.at[i],
            device_id=(dp, lax.rem(section + 1, sections)), device_id_type=MESH,
        )

    def backward_copy(i):
        rows = aligned(i, length)
        return pltpu.make_async_remote_copy(
            d_in.at[rows, :], grad.at[rows, :], backward_send.at[i], backward_recv.at[i],
            device_id=(dp, lax.rem(section + sections - 1, sections)), device_id_type=MESH,
        )

    def share_copy(source, target, i, away):
        owner = i // share
        remote = pltpu.make_async_remote_copy(
            source.at[aligned(i, length), :], target.at[aligned(lax.rem(i, share), length), :],
            share_send.at[away, i], share_recv.at[away, lax.rem(i, share)],
            device_id=(dp, owner), device_id_type=MESH,
        )
        local = pltpu.make_async_copy(
            source.at[aligned(i, length), :], target.at[aligned(lax.rem(i, share), length), :],
            share_recv.at[away, lax.rem(i, share)],
        )
        return owner, remote, local

    def send_share(source, target, i, away):
        owner, remote, local = share_copy(source, target, i, away)

        @pl.when(owner == section)
        def _():
            local.start()

        @pl.when(owner != section)
        def _():
            remote.start()

    def before_forward(i):
        @pl.when(section == 0)
        def _():
            load_rows(tokens, rows_in, i).wait()

        @pl.when(section > 0)
        def _():
            forward_copy(i).wait_recv()

    def after_forward(i):
        @pl.when(section < final)
        def _():
            forward_copy(i).start()

        @pl.when(section == final)
        def _():
            send_share(out, layer_out, i, 0)

    def before_backward(i):
        @pl.when(section == final)
        def _():
            load_rows(cotangent, grad, i).wait()

        @pl.when(section < final)
        def _():
            backward_copy(i).wait_recv()

    def after_backward(i):
        @pl.when(section > 0)
        def _():
            backward_copy(i).start()

        @pl.when(section == 0)
        def _():
            send_share(d_in, input_out, i, 1)

    lag = jnp.where(section == final, 0, jnp.where(section == final - 1, min(2, batches), batches))

    def ticks(forward, backward):
        def tick(t, carry):
            @pl.when(t < batches)
            def _():
                before_forward(t)
                forward(t)
                after_forward(t)

            late = t - lag

            @pl.when((late >= 0) & (late < batches))
            def _():
                before_backward(late)
                backward(late)
                after_backward(late)

            return carry

        lax.fori_loop(0, 2 * batches, tick, 0)

    def store(m, source, k):
        columns = aligned(k, width)
        return pltpu.make_async_copy(
            source.at[:, columns], weight_sums.at[m, :, columns], store_sem.at[m, k]
        )

    units = hidden // width

    @pl.when(is_attention)
    def _():
        load_weight.wait()
        for which in range(3):
            columns = slice(which * width, (which + 1) * width)
            down[:, columns] = weight[:, columns].T
        ticks(
            lambda i: attend_forward(i, gain, shift, refs),
            lambda i: attend_backward(i, gain, refs),
        )

        def unit(k, carry):
            columns = aligned(k, width)
            weight[:, columns] = dot_tn(rows_in[...], keep[:, columns]).astype(bf16)
            store(0, weight, k).start()
            return carry

        lax.fori_loop(0, units - 1, unit, 0)
        columns = slice(3 * width, 4 * width)
        weight[:, columns] = dot_tn(keep[:, columns], grad[...]).astype(bf16)
        store(0, weight, units - 1).start()

    @pl.when(is_feed)
    def _():
        load_weight.wait()
        load_down.wait()
        ticks(
            lambda i: feed_forward(aligned(i, length), gain, shift, refs),
            lambda i: feed_backward(aligned(i, length), gain, refs),
        )

        def unit(k, carry):
            columns = aligned(k, width)
            weight[:, columns] = dot_tn(rows_in[...], wide[:, columns]).astype(bf16)
            store(0, weight, k).start()
            down[:, columns] = dot_tn(grad[...], keep[:, columns]).astype(bf16)
            store(1, down, k).start()
            return carry

        lax.fori_loop(0, units, unit, 0)

    norm_out[...] = norm_sums[...]

    def drain(i, carry):
        @pl.when(section < final)
        def _():
            forward_copy(i).wait_send()

        @pl.when(section > 0)
        def _():
            backward_copy(i).wait_send()

        for away, source, target, sender in ((0, out, layer_out, final), (1, d_in, input_out, 0)):
            owner, remote, local = share_copy(source, target, i, away)

            @pl.when((section == sender) & (owner != section))
            def _():
                remote.wait_send()

            @pl.when(owner == section)
            def _():
                @pl.when(section == sender)
                def _():
                    local.wait()

                @pl.when(section != sender)
                def _():
                    remote.wait_recv()

        return carry

    lax.fori_loop(0, batches, drain, 0)
    for k in range(units):
        store(0, weight, k).wait()

    @pl.when(is_feed)
    def _():
        for k in range(units):
            store(1, down, k).wait()


def on_device(tokens, cotangent, segment_ids, first_weight, down_weight, ln_gain, ln_shift):
    sections = lax.axis_size("section")
    count, width = tokens.shape
    batches, length = segment_ids.shape
    hidden = first_weight.shape[2]
    units = hidden // width
    share = batches // sections
    any_space = pl.BlockSpec(memory_space=pl.ANY)
    vmem = pl.BlockSpec(memory_space=pltpu.VMEM)
    dma = pltpu.SemaphoreType.DMA
    layer_rows, input_rows, weight_sums, norm_sums = pl.pallas_call(
        functools.partial(pipeline, sections),
        out_shape=(
            jax.ShapeDtypeStruct((count // sections, width), bf16),
            jax.ShapeDtypeStruct((count // sections, width), bf16),
            jax.ShapeDtypeStruct((2, width, hidden), bf16),
            jax.ShapeDtypeStruct((2, 8, width), f32),
        ),
        in_specs=[any_space, any_space, vmem, any_space, any_space, vmem, vmem],
        out_specs=(any_space, any_space, any_space, vmem),
        scratch_shapes=[
            pltpu.VMEM((count, width), bf16),
            pltpu.VMEM((count, hidden), bf16),
            pltpu.VMEM((count, hidden), bf16),
            pltpu.VMEM((count, width), bf16),
            pltpu.VMEM((count, width), bf16),
            pltpu.VMEM((count, 1), f32),
            pltpu.VMEM((count, width), bf16),
            pltpu.VMEM((count, width), bf16),
            pltpu.VMEM((width, hidden), bf16),
            pltpu.VMEM((width, hidden), bf16),
            pltpu.VMEM((2, 8, width), f32),
            pltpu.VMEM((width, length), f32),
            pltpu.VMEM((batches * 16, length), f32),
            dma((2,)),
            dma((batches,)),
            dma((batches,)),
            dma((batches,)),
            dma((batches,)),
            dma((batches,)),
            dma((2, batches)),
            dma((2, share)),
            dma((2, units)),
        ],
        compiler_params=pltpu.CompilerParams(
            collective_id=0, has_side_effects=True, vmem_limit_bytes=64 * 2**20
        ),
    )(tokens, cotangent, segment_ids, first_weight, down_weight, ln_gain, ln_shift)
    has_down = lax.rem(lax.axis_index("section"), 2) == 1
    first_sum = lax.psum_scatter(weight_sums[0], "dp", scatter_dimension=1, tiled=True)
    down_sum = lax.psum_scatter(
        jnp.where(has_down, weight_sums[1], jnp.zeros_like(weight_sums[1])),
        "dp",
        scatter_dimension=1,
        tiled=True,
    )
    norm_sum = lax.psum_scatter(jnp.sum(norm_sums, axis=1), "dp", scatter_dimension=1, tiled=True)
    return (
        layer_rows,
        input_rows,
        first_sum.astype(f32)[None],
        down_sum.astype(f32)[None],
        norm_sum[0:1],
        norm_sum[1:2],
    )


def solution(mesh):
    return jax.shard_map(
        on_device,
        mesh=mesh,
        in_specs=(
            P("dp", None),
            P("dp", None),
            P("dp", None),
            P("section", None, None),
            P("section", None, None),
            P("section", None),
            P("section", None),
        ),
        out_specs=(
            P(("dp", "section"), None),
            P(("dp", "section"), None),
            P("section", None, "dp"),
            P("section", None, "dp"),
            P("section", "dp"),
            P("section", "dp"),
        ),
        check_vma=False,
    )
```

time: 1530 us -> 402 us (0.26); the launches traced: 1500 us -> 401 us
  waiting for transfers between devices: 767 us -> 233 us
  matrix products: 267 us -> 0 us
  other arithmetic: 224 us -> 11.1 us
  Pallas kernels: 0 us -> 122 us
  starting transfers between devices: 121 us -> 0.12 us
  local copies, waits for them, and re-layouts: 89.2 us -> 20.9 us
  loops' own time: 17.9 us -> 0 us
    reduce_scatter x4 -> x0, waiting for transfers between devices: 416 us -> none  [the longest x1 168 us: on_device(): lax.psum_scatter(gradient_sums[0][None], 'dp', scatter_dimension=2, tiled...]
    dot_general x28 -> x0, matrix products: 267 us -> none  [the longest x4 83.8 us: feed_forward(): jnp.einsum('rf,df->rd', hidden, down_rows, preferred_element_type=jnp.flo...]
    ppermute x14 -> x0, waiting for transfers between devices: 247 us -> none  [shifted(): return lax.ppermute(block, axis, route)]
    add x21 -> x0, other arithmetic: 166 us -> none  [one_tick(): running + addend]
    unnamed x8 -> x6, waiting for transfers between devices: 104 us -> 233 us
    pallas_call x0 -> x1, Pallas kernels: none -> 122 us  [on_device(): pl.pallas_call(functools.partial(pipeline, sections), out_shape=(jax.Shap...]
    ppermute x14 -> x0, starting transfers between devices: 121 us -> none  [shifted(): return lax.ppermute(block, axis, route)]
    dynamic_update_slice x21 -> x0, other arithmetic: 33.8 us -> none  [the longest x7 18.6 us: one_tick(): lax.dynamic_update_index_in_dim(saved_inputs, jnp.where(active, source, p...]
  transfers between devices with their start and end apart: 20 -> 3, of which waited for: 17 -> 3; matrix products, arithmetic and copies ran while one was open for 15% -> 6% of each run, Pallas kernels for 0% -> 0%
where the time goes in v1:
time: 402 us; the launch traced here: 401 us
  waiting for transfers between devices  233 us (58%)
  Pallas kernels  122 us (30%)
  local copies, waits for them, and re-layouts  20.9 us (5%)
  between operations  13.8 us (3%)
  other arithmetic  11.1 us (3%)
    unnamed x6, waiting for transfers between devices  233 us
    pallas_call x1, Pallas kernels, on_device(): pl.pallas_call(functools.partial(pipeline, sections), out_shape=(jax.Shap...  122 us
    unnamed x13, local copies, waits for them, and re-layouts  20 us
    select_n x1, other arithmetic, on_device(): jnp.where(has_down, weight_sums[1], jnp.zeros_like(weight_sums[1]))  8.05 us
  transfers between devices with their start and end apart: 3, of which 3 were waited for; matrix products, arithmetic and copies ran while one was open for 6% of the time, Pallas kernels for 0%

profile of v1, /device:TPU:1, one launch (start us, length us, event | category | flops | bytes accessed | tf_op | source)
XLA Modules:
  0.0 401.1 jit_solution(2901136816241700657)
XLA Ops:
  7.2 0.0 reduce-scatter.14.cloned.1.call-start
  7.2 122.0 %shard_map.118 = (bf16[512,768]{1,0:T(8,128)(2,1)}, bf16[512,768]{1,0:T(8,128)(2,1)}, bf16[2,768,3072]{2,1,0:T(8,128)(2,1)}, f32[2,8,768]{2,1,0:T(8,128)}) custom-call(bf16[2048,768]{1,0:T(8,128)(2,1)} %tokens.1, bf16[2048,768]{1,0:T(8,128)(2,1)} %cotangent.1, s32[8,256]{1,0:T(8,128)} %segments.1, bf16[1,768,3072]{2,1,0:T(8,128)(2,1)} %weight_in.1, ...), custom_call_target="tpu_custom_call" | custom-call | tf_op jit(solution)/shard_map/pallas_call | solution.py:516
  129.2 0.8 reduce_sum.9
  130.0 0.9 copy.17
  130.9 0.0 reduce-scatter.14.cloned.1.call-update
  131.0 0.0 reduce-scatter.12.cloned.1.call-start
  131.0 8.0 %select_bitcast_fusion = (bf16[768,3072]{1,0:T(8,128)(2,1)}, bf16[768,3072]{1,0:T(8,128)(2,1)}) fusion(bf16[2,768,3072]{2,1,0:T(8,128)(2,1)} %get-tuple-element.12, pred[]{:T(512)S(6)} %eq.3), kind=kLoop, calls=%fused_computation | loop fusion | flops 2359296 | bytes 18874368 | tf_op jit(solution)/shard_map/jit(_where)/select_n | solution.py:557
  139.1 6.7 %copy.15 = bf16[768,3072]{0,1:T(8,128)(2,1)} copy(bf16[768,3072]{1,0:T(8,128)(2,1)} %get-tuple-element.14) | data formatting | bytes 9437184
  145.7 0.0 reduce-scatter.12.cloned.1.call-update
  145.8 0.0 reduce-scatter.10.cloned.1.call-start
  145.8 6.7 %copy.13 = bf16[768,3072]{0,1:T(8,128)(2,1)} copy(bf16[768,3072]{1,0:T(8,128)(2,1)} %get-tuple-element.15) | data formatting | bytes 9437184
  152.5 0.0 reduce-scatter.10.cloned.1.call-update
  152.6 39.2 %reduce-scatter.14.cloned.1.call-done = f32[96,2]{1,0:T(8,128)} async-done(((f32[768,2]{1,0:T(8,128)}), f32[96,2]{1,0:T(8,128)}) %reduce-scatter.14.cloned.1.call-update) | async-done | bytes 784
  191.8 0.9 fusion
  192.8 0.6 copy.20
  193.3 0.6 copy.19
  193.9 97.7 %reduce-scatter.12.cloned.1.call-done = bf16[384,768]{1,0:T(8,128)(2,1)} async-done(((bf16[3072,768]{1,0:T(8,128)(2,1)}), bf16[384,768]{1,0:T(8,128)(2,1)}) %reduce-scatter.12.cloned.1.call-update) | async-done | bytes 589840
  291.7 1.4 copy.16
  293.0 1.1 bitcast_convert_fusion
  294.1 96.2 %reduce-scatter.10.cloned.1.call-done = bf16[384,768]{1,0:T(8,128)(2,1)} async-done(((bf16[3072,768]{1,0:T(8,128)(2,1)}), bf16[384,768]{1,0:T(8,128)(2,1)}) %reduce-scatter.10.cloned.1.call-update) | async-done | bytes 589840
  390.4 1.4 copy.14
  391.7 1.1 bitcast_convert_fusion.1
  392.8 0.9 copy.23
  393.7 0.9 copy.24
  (4 shorter events, 0.0 us)
Async XLA Ops:
  7.2 184.6 %reduce-scatter.14.cloned.1.call-start = ((), (), s32[]{:S(2)}) async-start(), calls=%async_computation.5 | async-start | bytes 442368
  131.0 160.7 %reduce-scatter.12.cloned.1.call-start = ((), (), s32[]{:S(2)}) async-start(), calls=%async_computation.4 | async-start | bytes 5308416
  145.8 244.6 %reduce-scatter.10.cloned.1.call-start = ((), (), s32[]{:S(2)}) async-start(), calls=%async_computation.3 | async-start | bytes 5308416
  152.5 240.3 %copy-start.1 = (bf16[512,768]{1,0:T(8,128)(2,1)S(1)}, bf16[512,768]{1,0:T(8,128)(2,1)}, u32[]{:S(2)}) copy-start(bf16[512,768]{1,0:T(8,128)(2,1)} %get-tuple-element.24) | copy-start | bytes 2359300
  152.6 241.2 %copy-start = (bf16[512,768]{1,0:T(8,128)(2,1)S(1)}, bf16[512,768]{1,0:T(8,128)(2,1)}, u32[]{:S(2)}) copy-start(bf16[512,768]{1,0:T(8,128)(2,1)} %get-tuple-element.25) | copy-start | bytes 2359300
Sparse Core Ops, SparseCore 0:
  131.1 60.6 reduce-scatter.13
  195.4 96.1 reduce-scatter.11
  295.3 94.9 reduce-scatter.9

commit v2 on v1

--- a/solution.py
+++ b/solution.py
@@ -188,12 +188,12 @@
     rows = aligned(index, length)
     first_row = index * length
     d_resid = norm_backward(rows, gain, refs)
-    refs.d_context[...] = dot_nt(refs.weight[:, 3 * width :], d_resid.astype(bf16))
+    refs.d_context[:, :length] = dot_nt(refs.weight[:, 3 * width :], d_resid.astype(bf16))
     place = functools.partial(head_part, refs, first_row, length, blocks)
 
     def first(n):
         inverse = refs.inverse[pl.ds(index * 16 + n, 1), :]
-        d_context = refs.d_context[n * head_width : (n + 1) * head_width, :] * inverse
+        d_context = refs.d_context[n * head_width : (n + 1) * head_width, :length] * inverse
         along = jnp.sum(d_context * refs.keep[place(3, n)].astype(f32), axis=0, keepdims=True)
         d_context = d_context.astype(bf16)
         return dot_tn(refs.keep[place(2, n)], d_context), along, d_context
@@ -238,6 +238,7 @@
 
 def pipeline(
     sections,
+    levels,
     tokens,
     cotangent,
     segments,
@@ -247,7 +248,8 @@
     shift_in,
     layer_out,
     input_out,
-    weight_sums,
+    first_out,
+    down_out,
     norm_out,
     rows_in,
     keep,
@@ -271,6 +273,13 @@
     share_send,
     share_recv,
     store_sem,
+    level_recv=None,
+    norm_recv=None,
+    norm_send=None,
+    ready_sem=None,
+    pair_sems=None,
+    level_sems=None,
+    norm_sems=None,
 ):
     dp = lax.axis_index("dp")
     section = lax.axis_index("section")
@@ -312,7 +321,16 @@
         pl.semaphore_signal(
             barrier, inc=1, device_id=(dp, lax.rem(section + other, sections)), device_id_type=MESH
         )
-    pl.semaphore_wait(barrier, sections - 1)
+    if levels:
+        pair, level = lax.rem(dp, 2), dp // 2
+        partner = dp + 1 - 2 * pair
+        pl.semaphore_signal(barrier, inc=1, device_id=(partner, section), device_id_type=MESH)
+        peers = [lax.rem(dp + 2 * other, 2 * levels) for other in range(1, levels)]
+        for peer in peers:
+            pl.semaphore_signal(barrier, inc=1, device_id=(peer, section), device_id_type=MESH)
+        pl.semaphore_wait(barrier, sections - 1 + levels)
+    else:
+        pl.semaphore_wait(barrier, sections - 1)
 
     norm_sums[...] = jnp.zeros_like(norm_sums)
     gain = gain_in[...]
@@ -370,10 +388,6 @@
         def _():
             forward_copy(i).start()
 
-        @pl.when(section == final)
-        def _():
-            send_share(out, layer_out, i, 0)
-
     def before_backward(i):
         @pl.when(section == final)
         def _():
@@ -393,37 +407,316 @@
             send_share(d_in, input_out, i, 1)
 
     lag = jnp.where(section == final, 0, jnp.where(section == final - 1, min(2, batches), batches))
+
+    mask = (1 << (batches - 1).bit_length()) - 1
 
     def ticks(forward, backward):
         def tick(t, carry):
             @pl.when(t < batches)
             def _():
-                before_forward(t)
-                forward(t)
-                after_forward(t)
+                i = t & mask
+                before_forward(i)
+                forward(i)
+                after_forward(i)
 
             late = t - lag
 
             @pl.when((late >= 0) & (late < batches))
             def _():
-                before_backward(late)
-                backward(late)
-                after_backward(late)
+                i = late & mask
+                before_backward(i)
+                backward(i)
+                after_backward(i)
 
             return carry
 
         lax.fori_loop(0, 2 * batches, tick, 0)
 
-    def store(m, source, k):
-        columns = aligned(k, width)
-        return pltpu.make_async_copy(
-            source.at[:, columns], weight_sums.at[m, :, columns], store_sem.at[m, k]
-        )
-
     units = hidden // width
+
+    def gradient_rows_left():
+        @pl.when(section > 0)
+        def _():
+            def one(i, carry):
+                backward_copy(i).wait_send()
+                return carry
+
+            lax.fori_loop(0, batches, one, 0)
+
+    def send_output():
+        @pl.when(section == final)
+        def _():
+            def one(i, carry):
+                send_share(out, layer_out, i, 0)
+                return carry
+
+            lax.fori_loop(0, batches, one, 0)
+
+    def drain():
+        def one(i, carry):
+            @pl.when(section < final)
+            def _():
+                forward_copy(i).wait_send()
+
+            @pl.when((section > 0) & is_attention)
+            def _():
+                backward_copy(i).wait_send()
+
+            for away, source, target, sender in ((0, out, layer_out, final), (1, d_in, input_out, 0)):
+                owner, remote, local = share_copy(source, target, i, away)
+
+                @pl.when((section == sender) & (owner != section))
+                def _():
+                    remote.wait_send()
+
+                @pl.when((section == sender) & (owner == section))
+                def _():
+                    local.wait()
+
+                @pl.when((section != sender) & (owner == section))
+                def _():
+                    remote.wait_recv()
+
+            return carry
+
+        lax.fori_loop(0, batches, one, 0)
+
+    def plain_gradients(parts, late, line_first=()):
+        def store(m, source, target, k):
+            columns = aligned(k, width)
+            return pltpu.make_async_copy(
+                source.at[:, columns], target.at[:, columns], store_sem.at[m, k]
+            )
+
+        for m, (make, source, _, target) in enumerate(parts):
+
+            def unit(k, carry):
+                make(k)
+                store(m, source, target, k).start()
+                return carry
+
+            lax.fori_loop(0, units, unit, 0)
+        send_output()
+        norm_out[...] = jnp.sum(norm_sums[...], axis=1)
+        for m, (make, source, _, target) in enumerate(parts):
+            for k in range(units):
+                store(m, source, target, k).wait()
+
+    def summed_gradients(parts, late, line_first=()):
+        columns_out = hidden // (2 * levels)
+        halves = 2
+        part_rows = width // halves
+
+        above, below = levels - 1 - level, level
+
+        def level_of(j):
+            near_low = jnp.where(j < above, levels - 1 - j, j - above)
+            near_high = jnp.where(j < below, j, levels - 1 - (j - below))
+            moving = jnp.where(level < levels // 2, near_low, near_high)
+            return jnp.where(j == levels - 1, level, moving)
+
+        def half_of(source, k, side, h):
+            column = pl.multiple_of(k * width + side * columns_out, columns_out)
+            return source.at[pl.ds(h * part_rows, part_rows), pl.ds(column, columns_out)]
+
+        def pair_slot(landing, k, h):
+            row = pl.multiple_of((k // 2) * width + h * part_rows, part_rows)
+            column = pl.multiple_of(lax.rem(k, 2) * columns_out, columns_out)
+            return landing.at[pl.ds(row, part_rows), pl.ds(column, columns_out)]
+
+        def pair_copy(m, k, h):
+            _, source, landing, _ = parts[m]
+            return pltpu.make_async_remote_copy(
+                half_of(source, k, 1 - pair, h), pair_slot(landing, k, h),
+                pair_sems.at[0, m, k, h], pair_sems.at[1, m, k, h],
+                device_id=(partner, section), device_id_type=MESH,
+            )
+
+        def level_slot(m, slot, h):
+            return level_recv.at[m, slot, pl.ds(h * part_rows, part_rows), :]
+
+        def level_copy(m, k, h, other=False):
+            step = jnp.where(k > level, 1, -1)
+            slot = jnp.where(k == level - 1, levels, k)
+            side = 1 - pair if other else pair
+            place = 1 if other else m
+            return pltpu.make_async_remote_copy(
+                half_of(parts[m][1], k, side, h), level_slot(place, slot, h),
+                level_sems.at[0, place, k, h], level_sems.at[1, place, slot, h],
+                device_id=(dp + 2 * step, section), device_id_type=MESH,
+            )
+
+        def arrival(m, slot, h):
+            return pltpu.make_async_copy(
+                level_slot(m, slot, h), level_slot(m, slot, h), level_sems.at[1, m, slot, h]
+            )
+
+        def make_unit(m, k):
+            parts[m][0](k)
+            for h in range(halves):
+                if h not in line_first:
+                    pair_copy(m, k, h).start()
+
+        def pass_on(m, k, h, mine, total, other=False):
+            from_below = (k > level) & (level > 0)
+            from_above = (k < level) & (level < levels - 1)
+            moving = from_below | from_above
+            place = 1 if other else m
+
+            @pl.when(moving)
+            def _():
+                arrival(place, k, h).wait()
+                mine[...] = (total() + level_slot(place, k, h)[...].astype(f32)).astype(bf16)
+
+            @pl.when(jnp.logical_not(moving))
+            def _():
+                mine[...] = total().astype(bf16)
+
+            @pl.when(k != level)
+            def _():
+                level_copy(m, k, h, other).start()
+
+        def pass_unit(m, k):
+            _, source, landing, _ = parts[m]
+            for h in line_first:
+
+                @pl.when(k != level)
+                def _():
+                    for other in (False, True):
+                        mine = half_of(source, k, 1 - pair if other else pair, h)
+                        pass_on(m, k, h, mine, lambda: mine[...].astype(f32), other)
+
+            for h in range(halves):
+                if h in line_first:
+                    continue
+                pair_copy(m, k, h).wait_recv()
+                mine = half_of(source, k, pair, h)
+                theirs = pair_slot(landing, k, h)
+                pass_on(m, k, h, mine, lambda: mine[...].astype(f32) + theirs[...].astype(f32))
+
+        def gather(m, h, other=False):
+            place = 1 if other else m
+            side = 1 - pair if other else pair
+            wanted = d_context.at[pl.ds(h * part_rows, part_rows), pl.ds(0, columns_out)]
+            wanted[...] = half_of(parts[m][1], level, side, h)[...].astype(f32)
+            for there, slot in ((level > 0, level), (level < levels - 1, levels)):
+
+                @pl.when(there)
+                def _():
+                    arrival(place, slot, h).wait()
+                    wanted[...] += level_slot(place, slot, h)[...].astype(f32)
+
+            return wanted
+
+        def last_unit(m):
+            _, source, landing, target = parts[m]
+            for h in line_first:
+                half_of(source, level, 1 - pair, h)[...] = gather(m, h, True)[...].astype(bf16)
+                pair_copy(m, level, h).start()
+            copies = []
+            for h in [h for h in range(halves) if h not in line_first] + list(line_first):
+                wanted = gather(m, h)
+                if h in line_first:
+                    pair_copy(m, level, h).wait_recv()
+                    wanted[...] += pair_slot(landing, level, h)[...].astype(f32)
+                rows = pl.ds(h * part_rows, part_rows)
+                copies.append(pltpu.make_async_copy(wanted, target.at[0, rows, :], store_sem.at[m, h]))
+                copies[-1].start()
+            for copy in copies:
+                copy.wait()
+
+        def norm_copy(way, device):
+            return pltpu.make_async_remote_copy(
+                norm_send.at[min(way, 1)], norm_recv.at[way], norm_sems.at[0, way], norm_sems.at[1, way],
+                device_id=(device, section), device_id_type=MESH,
+            )
+
+        def start_norms():
+            norm_send[0] = jnp.concatenate(
+                [jnp.sum(norm_sums[...], axis=1), jnp.zeros((6, width), f32)], axis=0
+            )
+            norm_copy(0, partner).start()
+
+        def spread_norms():
+            norm_copy(0, partner).wait_recv()
+            norm_send[1] = norm_send[0] + norm_recv[0]
+            for way, peer in enumerate(peers, 1):
+                norm_copy(way, peer).start()
+
+        def finish_norms():
+            total = norm_send[1]
+            for way, peer in enumerate(peers, 1):
+                norm_copy(way, peer).wait_recv()
+                total = total + norm_recv[way]
+            norm_out[...] = total
+            norm_copy(0, partner).wait_send()
+            for way, peer in enumerate(peers, 1):
+                norm_copy(way, peer).wait_send()
+
+        start_norms()
+        pl.semaphore_signal(ready_sem, inc=1, device_id=(partner, section), device_id_type=MESH)
+        pl.semaphore_wait(ready_sem, 1)
+        total_units = len(parts) * units
+
+        def of_unit(t, act):
+            for m in range(len(parts)):
+
+                @pl.when(t // units == m)
+                def _():
+                    act(m, level_of(lax.rem(t, units)))
+
+        def turn(t, carry):
+            @pl.when(t < total_units)
+            def _():
+                of_unit(t, make_unit)
+
+            @pl.when(t == 0)
+            def _():
+                spread_norms()
+
+            @pl.when(t >= late)
+            def _():
+                of_unit(t - late, pass_unit)
+
+            return carry
+
+        lax.fori_loop(0, total_units, turn, 0)
+        send_output()
+        lax.fori_loop(total_units, total_units + late, turn, 0)
+        for m in range(len(parts)):
+            last_unit(m)
+        finish_norms()
+
+        def sent(k, carry):
+            for m in range(len(parts)):
+                for h in range(halves):
+                    if h not in line_first:
+                        pair_copy(m, k, h).wait_send()
+
+                    @pl.when(k != level)
+                    def _():
+                        level_copy(m, k, h).wait_send()
+                        if h in line_first:
+                            level_copy(m, k, h, True).wait_send()
+
+            return carry
+
+        lax.fori_loop(0, units, sent, 0)
+        for m in range(len(parts)):
+            for h in line_first:
+                pair_copy(m, level, h).wait_send()
+
+    weight_gradients = summed_gradients if levels else plain_gradients
 
     @pl.when(is_attention)
     def _():
+        if levels:
+            d_context[...] = jnp.zeros_like(d_context)
+            zeros = pltpu.make_async_copy(
+                d_context.at[:, pl.ds(0, hidden // (2 * levels))], down_out.at[0], load_sem.at[1]
+            )
+            zeros.start()
+            zeros.wait()
         load_weight.wait()
         for which in range(3):
             columns = slice(which * width, (which + 1) * width)
@@ -433,16 +726,18 @@
             lambda i: attend_backward(i, gain, refs),
         )
 
-        def unit(k, carry):
+        def first(k):
             columns = aligned(k, width)
-            weight[:, columns] = dot_tn(rows_in[...], keep[:, columns]).astype(bf16)
-            store(0, weight, k).start()
-            return carry
-
-        lax.fori_loop(0, units - 1, unit, 0)
-        columns = slice(3 * width, 4 * width)
-        weight[:, columns] = dot_tn(keep[:, columns], grad[...]).astype(bf16)
-        store(0, weight, units - 1).start()
+
+            @pl.when(k < units - 1)
+            def _():
+                weight[:, columns] = dot_tn(rows_in[...], keep[:, columns]).astype(bf16)
+
+            @pl.when(k == units - 1)
+            def _():
+                weight[:, columns] = dot_tn(keep[:, columns], grad[...]).astype(bf16)
+
+        weight_gradients(((first, weight, normal, first_out),), 1, (0,))
 
     @pl.when(is_feed)
     def _():
@@ -453,121 +748,102 @@
             lambda i: feed_backward(aligned(i, length), gain, refs),
         )
 
-        def unit(k, carry):
+        gradient_rows_left()
+
+        def first(k):
             columns = aligned(k, width)
             weight[:, columns] = dot_tn(rows_in[...], wide[:, columns]).astype(bf16)
-            store(0, weight, k).start()
+
+        def second(k):
+            columns = aligned(k, width)
             down[:, columns] = dot_tn(grad[...], keep[:, columns]).astype(bf16)
-            store(1, down, k).start()
-            return carry
-
-        lax.fori_loop(0, units, unit, 0)
-
-    norm_out[...] = norm_sums[...]
-
-    def drain(i, carry):
-        @pl.when(section < final)
-        def _():
-            forward_copy(i).wait_send()
-
-        @pl.when(section > 0)
-        def _():
-            backward_copy(i).wait_send()
-
-        for away, source, target, sender in ((0, out, layer_out, final), (1, d_in, input_out, 0)):
-            owner, remote, local = share_copy(source, target, i, away)
-
-            @pl.when((section == sender) & (owner != section))
-            def _():
-                remote.wait_send()
-
-            @pl.when(owner == section)
-            def _():
-                @pl.when(section == sender)
-                def _():
-                    local.wait()
-
-                @pl.when(section != sender)
-                def _():
-                    remote.wait_recv()
-
-        return carry
-
-    lax.fori_loop(0, batches, drain, 0)
-    for k in range(units):
-        store(0, weight, k).wait()
-
-    @pl.when(is_feed)
-    def _():
-        for k in range(units):
-            store(1, down, k).wait()
+
+        weight_gradients(
+            ((first, weight, normal, first_out), (second, down, d_in, down_out)), 2
+        )
+
+    drain()
 
 
 def on_device(tokens, cotangent, segment_ids, first_weight, down_weight, ln_gain, ln_shift):
     sections = lax.axis_size("section")
+    groups = lax.axis_size("dp")
     count, width = tokens.shape
     batches, length = segment_ids.shape
     hidden = first_weight.shape[2]
     units = hidden // width
     share = batches // sections
+    levels = units if groups == 2 * units and (units + 1) // 2 * width <= count else 0
+    columns_out = hidden // groups
     any_space = pl.BlockSpec(memory_space=pl.ANY)
     vmem = pl.BlockSpec(memory_space=pltpu.VMEM)
     dma = pltpu.SemaphoreType.DMA
-    layer_rows, input_rows, weight_sums, norm_sums = pl.pallas_call(
-        functools.partial(pipeline, sections),
+    if levels:
+        sums = [jax.ShapeDtypeStruct((1, width, columns_out), f32)] * 2
+        sums.append(jax.ShapeDtypeStruct((8, width), f32))
+    else:
+        sums = [jax.ShapeDtypeStruct((width, hidden), bf16)] * 2
+        sums.append(jax.ShapeDtypeStruct((2, width), f32))
+    scratch = [
+        pltpu.VMEM((count, width), bf16),
+        pltpu.VMEM((count, hidden), bf16),
+        pltpu.VMEM((count, hidden), bf16),
+        pltpu.VMEM((count, width), bf16),
+        pltpu.VMEM((count, width), bf16),
+        pltpu.VMEM((count, 1), f32),
+        pltpu.VMEM((count, width), bf16),
+        pltpu.VMEM((count, width), bf16),
+        pltpu.VMEM((width, hidden), bf16),
+        pltpu.VMEM((width, hidden), bf16),
+        pltpu.VMEM((2, 8, width), f32),
+        pltpu.VMEM((width, max(length, columns_out if levels else 0)), f32),
+        pltpu.VMEM((batches * 16, length), f32),
+        dma((2,)),
+        dma((batches,)),
+        dma((batches,)),
+        dma((batches,)),
+        dma((batches,)),
+        dma((batches,)),
+        dma((2, batches)),
+        dma((2, share)),
+        dma((2, units)),
+    ]
+    if levels:
+        scratch += [
+            pltpu.VMEM((2, levels + 1, width, columns_out), bf16),
+            pltpu.VMEM((levels, 8, width), f32),
+            pltpu.VMEM((2, 8, width), f32),
+            pltpu.SemaphoreType.REGULAR,
+            dma((2, 2, levels, 2)),
+            dma((2, 2, levels + 1, 2)),
+            dma((2, levels)),
+        ]
+    layer_rows, input_rows, first_sum, down_sum, norm_sum = pl.pallas_call(
+        functools.partial(pipeline, sections, levels),
         out_shape=(
             jax.ShapeDtypeStruct((count // sections, width), bf16),
             jax.ShapeDtypeStruct((count // sections, width), bf16),
-            jax.ShapeDtypeStruct((2, width, hidden), bf16),
-            jax.ShapeDtypeStruct((2, 8, width), f32),
+            *sums,
         ),
         in_specs=[any_space, any_space, vmem, any_space, any_space, vmem, vmem],
-        out_specs=(any_space, any_space, any_space, vmem),
-        scratch_shapes=[
-            pltpu.VMEM((count, width), bf16),
-            pltpu.VMEM((count, hidden), bf16),
-            pltpu.VMEM((count, hidden), bf16),
-            pltpu.VMEM((count, width), bf16),
-            pltpu.VMEM((count, width), bf16),
-            pltpu.VMEM((count, 1), f32),
-            pltpu.VMEM((count, width), bf16),
-            pltpu.VMEM((count, width), bf16),
-            pltpu.VMEM((width, hidden), bf16),
-            pltpu.VMEM((width, hidden), bf16),
-            pltpu.VMEM((2, 8, width), f32),
-            pltpu.VMEM((width, length), f32),
-            pltpu.VMEM((batches * 16, length), f32),
-            dma((2,)),
-            dma((batches,)),
-            dma((batches,)),
-            dma((batches,)),
-            dma((batches,)),
-            dma((batches,)),
-            dma((2, batches)),
-            dma((2, share)),
-            dma((2, units)),
-        ],
+        out_specs=(any_space, any_space, any_space, any_space, vmem),
+        scratch_shapes=scratch,
         compiler_params=pltpu.CompilerParams(
             collective_id=0, has_side_effects=True, vmem_limit_bytes=64 * 2**20
         ),
     )(tokens, cotangent, segment_ids, first_weight, down_weight, ln_gain, ln_shift)
-    has_down = lax.rem(lax.axis_index("section"), 2) == 1
-    first_sum = lax.psum_scatter(weight_sums[0], "dp", scatter_dimension=1, tiled=True)
-    down_sum = lax.psum_scatter(
-        jnp.where(has_down, weight_sums[1], jnp.zeros_like(weight_sums[1])),
-        "dp",
-        scatter_dimension=1,
-        tiled=True,
-    )
-    norm_sum = lax.psum_scatter(jnp.sum(norm_sums, axis=1), "dp", scatter_dimension=1, tiled=True)
-    return (
-        layer_rows,
-        input_rows,
-        first_sum.astype(f32)[None],
-        down_sum.astype(f32)[None],
-        norm_sum[0:1],
-        norm_sum[1:2],
-    )
+    if levels:
+        own = width // groups
+        norm_sum = lax.dynamic_slice_in_dim(norm_sum, lax.axis_index("dp") * own, own, 1)
+    else:
+        has_down = lax.rem(lax.axis_index("section"), 2) == 1
+        down_sum = jnp.where(has_down, down_sum, jnp.zeros_like(down_sum))
+        first_sum, down_sum, norm_sum = (
+            lax.psum_scatter(value, "dp", scatter_dimension=1, tiled=True)
+            for value in (first_sum, down_sum, norm_sum)
+        )
+        first_sum, down_sum = first_sum.astype(f32)[None], down_sum.astype(f32)[None]
+    return (layer_rows, input_rows, first_sum, down_sum, norm_sum[0:1], norm_sum[1:2])
 
 
 def solution(mesh):

time: 402 us -> 184 us (0.46)
  waiting for transfers between devices: 233 us -> 0 us
  Pallas kernels: 122 us -> 176 us
  local copies, waits for them, and re-layouts: 20.9 us -> 7.61 us
  between operations: 13.8 us -> 0.67 us
  other arithmetic: 11.1 us -> 0 us
    unnamed x6 -> x0, waiting for transfers between devices: 233 us -> none
    pallas_call x1, Pallas kernels: 122 us -> 176 us  [on_device(): pl.pallas_call(functools.partial(pipeline, sections, levels), out_shape=(...]
    unnamed x13 -> x8, local copies, waits for them, and re-layouts: 20 us -> 6.16 us
    select_n x1 -> x0, other arithmetic: 8.05 us -> none  [on_device(): jnp.where(has_down, weight_sums[1], jnp.zeros_like(weight_sums[1]))]
  transfers between devices with their start and end apart: 3 -> 0, of which waited for: 3 -> 0; matrix products, arithmetic and copies ran while one was open for 6% -> 0% of each run, Pallas kernels for 0% -> 0%
where the time goes in v2:
time: 184 us
  Pallas kernels  176 us (96%)
  local copies, waits for them, and re-layouts  7.61 us (4%)
    pallas_call x1, Pallas kernels, on_device(): pl.pallas_call(functools.partial(pipeline, sections, levels), out_shape=(...  176 us
    unnamed x8, local copies, waits for them, and re-layouts  6.16 us

profile of v2, /device:TPU:1, one launch (start us, length us, event | category | flops | bytes accessed | tf_op | source)
XLA Modules:
  0.0 184.2 jit_solution(1007196493117817470)
XLA Ops:
  0.6 175.9 %shard_map.118 = (bf16[512,768]{1,0:T(8,128)(2,1)}, bf16[512,768]{1,0:T(8,128)(2,1)}, f32[1,768,384]{2,1,0:T(8,128)}, f32[1,768,384]{2,1,0:T(8,128)}, f32[8,768]{1,0:T(8,128)}) custom-call(bf16[2048,768]{1,0:T(8,128)(2,1)} %tokens.1, bf16[2048,768]{1,0:T(8,128)(2,1)} %cotangent.1, s32[8,256]{1,0:T(8,128)} %segments.1, bf16[1,768,3072]{2,1,0:T(8,128)(2,1)} %weight_in.1, ...), custom_call_target="tpu_custom_call" | custom-call | tf_op jit(solution)/shard_map/pallas_call | solution.py:821
  176.6 0.0 copy-start.1
  176.6 0.0 copy-start
  176.6 0.9 constant_dynamic-slice_fusion
  177.5 0.5 fusion
  178.1 2.1 %copy.17 = bf16[512,768]{1,0:T(8,128)(2,1)} copy(bf16[512,768]{1,0:T(8,128)(2,1)} %get-tuple-element.24) | data formatting | bytes 1572864
  180.1 2.1 %copy.18 = bf16[512,768]{1,0:T(8,128)(2,1)} copy(bf16[512,768]{1,0:T(8,128)(2,1)} %get-tuple-element.25) | data formatting | bytes 1572864
  182.2 0.0 copy-done.1
  182.2 1.0 copy.19
  183.2 0.0 copy-done
  183.2 1.0 copy.20
Async XLA Ops:
  176.6 5.6 %copy-start.1 = (f32[1,768,384]{2,1,0:T(8,128)S(1)}, f32[1,768,384]{2,1,0:T(8,128)}, u32[]{:S(2)}) copy-start(f32[1,768,384]{2,1,0:T(8,128)} %get-tuple-element.26) | copy-start | bytes 3538948
  176.6 6.6 %copy-start = (f32[1,768,384]{2,1,0:T(8,128)S(1)}, f32[1,768,384]{2,1,0:T(8,128)}, u32[]{:S(2)}) copy-start(f32[1,768,384]{2,1,0:T(8,128)} %get-tuple-element.27) | copy-start | bytes 3538948

commit v3 on v2

--- a/solution.py
+++ b/solution.py
@@ -8,6 +8,7 @@
 from jax.sharding import PartitionSpec as P
 
 HEADS = 12
+HALVES = 4
 NORM_EPSILON = 1e-12
 MASKED_SCORE = -1e30
 INV_SQRT2 = 0.7071067811865476
@@ -157,7 +158,7 @@
         refs.inverse[pl.ds(index * 16 + n, 1), :] = inverse
         refs.keep[place(3, n)] = (dot(refs.keep[place(2, n)], raw) * inverse).astype(bf16)
 
-    ahead = 2
+    ahead = 3
     scores = [score(n) for n in range(ahead)]
     held = None
     for n in range(HEADS):
@@ -188,12 +189,25 @@
     rows = aligned(index, length)
     first_row = index * length
     d_resid = norm_backward(rows, gain, refs)
-    refs.d_context[:, :length] = dot_nt(refs.weight[:, 3 * width :], d_resid.astype(bf16))
+    d_branch = d_resid.astype(bf16)
+    total = d_resid
+
+    def unmix(j):
+        some = slice(j * length, (j + 1) * length)
+        refs.d_context[some, :] = dot_nt(refs.weight[some, 3 * width :], d_branch)
+
+    def unproject(j):
+        some = [slice((which * blocks + j) * length, (which * blocks + j + 1) * length) for which in range(3)]
+        left = jnp.concatenate([refs.keep[rows, part] for part in some], axis=1)
+        right = jnp.concatenate([refs.weight[:, part] for part in some], axis=1)
+        return dot_nt(left, right)
+
+    unmix(0)
     place = functools.partial(head_part, refs, first_row, length, blocks)
 
     def first(n):
         inverse = refs.inverse[pl.ds(index * 16 + n, 1), :]
-        d_context = refs.d_context[n * head_width : (n + 1) * head_width, :length] * inverse
+        d_context = refs.d_context[n * head_width : (n + 1) * head_width, :] * inverse
         along = jnp.sum(d_context * refs.keep[place(3, n)].astype(f32), axis=0, keepdims=True)
         d_context = d_context.astype(bf16)
         return dot_tn(refs.keep[place(2, n)], d_context), along, d_context
@@ -221,13 +235,18 @@
     current = first(0)
     held = None
     for n in range(HEADS):
+        j, place_in = n // per_block, n % per_block
+        if place_in == 1 and j + 1 < blocks:
+            unmix(j + 1)
         following = first(n + 1) if n + 1 < HEADS else None
         ready = second(n, *current)
         if held is not None:
             third(n - 1, *held)
+        if place_in == 2 and j > 0:
+            total = total + unproject(j - 1)
         held, current = ready, following
     third(HEADS - 1, *held)
-    d_in = d_resid + dot_nt(refs.keep[rows, : 3 * width], refs.weight[:, : 3 * width])
+    d_in = total + unproject(blocks - 1)
     refs.d_in[rows, :] = d_in.astype(bf16)
 
 
@@ -241,7 +260,7 @@
     levels,
     tokens,
     cotangent,
-    segments,
+    segments_in,
     weight_in,
     down_in,
     gain_in,
@@ -264,6 +283,8 @@
     norm_sums,
     d_context,
     inverse,
+    segments,
+    gains,
     load_sem,
     first_sem,
     forward_send,
@@ -273,6 +294,7 @@
     share_send,
     share_recv,
     store_sem,
+    stage=None,
     level_recv=None,
     norm_recv=None,
     norm_send=None,
@@ -298,9 +320,23 @@
         rows = aligned(i, length)
         return pltpu.make_async_copy(source.at[rows, :], target.at[rows, :], first_sem.at[i])
 
-    load_weight = pltpu.make_async_copy(weight_in.at[0], weight, load_sem.at[0])
-    load_down = pltpu.make_async_copy(down_in.at[0], down, load_sem.at[1])
-    load_weight.start()
+    def load_weight(part):
+        columns = slice(part * width, (part + 1) * width)
+        return pltpu.make_async_copy(weight_in.at[0, :, columns], weight.at[:, columns], load_sem.at[part])
+
+    units = hidden // width
+    load_down = pltpu.make_async_copy(down_in.at[0], down, load_sem.at[units])
+    small = [
+        pltpu.make_async_copy(source, target, load_sem.at[units + 1 + i])
+        for i, (source, target) in enumerate(
+            ((segments_in, segments), (gain_in, gains.at[0]), (shift_in, gains.at[1]))
+        )
+    ]
+    load_weight(0).start()
+    for copy in small:
+        copy.start()
+    for part in range(1, units):
+        load_weight(part).start()
 
     @pl.when(is_feed)
     def _():
@@ -328,13 +364,14 @@
         peers = [lax.rem(dp + 2 * other, 2 * levels) for other in range(1, levels)]
         for peer in peers:
             pl.semaphore_signal(barrier, inc=1, device_id=(peer, section), device_id_type=MESH)
+    norm_sums[...] = jnp.zeros_like(norm_sums)
+    for copy in small:
+        copy.wait()
+    gain = gains[0]
+    shift = gains[1]
+
+    def meet():
         pl.semaphore_wait(barrier, sections - 1 + levels)
-    else:
-        pl.semaphore_wait(barrier, sections - 1)
-
-    norm_sums[...] = jnp.zeros_like(norm_sums)
-    gain = gain_in[...]
-    shift = shift_in[...]
 
     def forward_copy(i):
         rows = aligned(i, length)
@@ -491,7 +528,7 @@
         for m, (make, source, _, target) in enumerate(parts):
 
             def unit(k, carry):
-                make(k)
+                make(k, slice(0, width))
                 store(m, source, target, k).start()
                 return carry
 
@@ -504,7 +541,7 @@
 
     def summed_gradients(parts, late, line_first=()):
         columns_out = hidden // (2 * levels)
-        halves = 2
+        halves = HALVES
         part_rows = width // halves
 
         above, below = levels - 1 - level, level
@@ -551,11 +588,22 @@
                 level_slot(m, slot, h), level_slot(m, slot, h), level_sems.at[1, m, slot, h]
             )
 
-        def make_unit(m, k):
-            parts[m][0](k)
-            for h in range(halves):
+        def send_pair(m, k, some):
+            for h in some:
                 if h not in line_first:
                     pair_copy(m, k, h).start()
+
+        def make_unit(m, k, t):
+            for g in range(2):
+                parts[m][0](k, slice(g * width // 2, (g + 1) * width // 2))
+                if not line_first:
+                    if g == 0:
+
+                        @pl.when(lax.rem(t, units) == 0)
+                        def _():
+                            pl.semaphore_wait(ready_sem.at[m], 1)
+
+                    send_pair(m, k, range(g * halves // 2, (g + 1) * halves // 2))
 
         def pass_on(m, k, h, mine, total, other=False):
             from_below = (k > level) & (level > 0)
@@ -576,8 +624,8 @@
             def _():
                 level_copy(m, k, h, other).start()
 
-        def pass_unit(m, k):
-            _, source, landing, _ = parts[m]
+        def pass_line(m, k, t):
+            source = parts[m][1]
             for h in line_first:
 
                 @pl.when(k != level)
@@ -586,6 +634,8 @@
                         mine = half_of(source, k, 1 - pair if other else pair, h)
                         pass_on(m, k, h, mine, lambda: mine[...].astype(f32), other)
 
+        def pass_pair(m, k, t):
+            _, source, landing, _ = parts[m]
             for h in range(halves):
                 if h in line_first:
                     continue
@@ -597,7 +647,7 @@
         def gather(m, h, other=False):
             place = 1 if other else m
             side = 1 - pair if other else pair
-            wanted = d_context.at[pl.ds(h * part_rows, part_rows), pl.ds(0, columns_out)]
+            wanted = stage.at[pl.ds(h * part_rows, part_rows), :]
             wanted[...] = half_of(parts[m][1], level, side, h)[...].astype(f32)
             for there, slot in ((level > 0, level), (level < levels - 1, levels)):
 
@@ -608,11 +658,13 @@
 
             return wanted
 
+        def last_line(m):
+            for h in line_first:
+                half_of(parts[m][1], level, 1 - pair, h)[...] = gather(m, h, True)[...].astype(bf16)
+                pair_copy(m, level, h).start()
+
         def last_unit(m):
             _, source, landing, target = parts[m]
-            for h in line_first:
-                half_of(source, level, 1 - pair, h)[...] = gather(m, h, True)[...].astype(bf16)
-                pair_copy(m, level, h).start()
             copies = []
             for h in [h for h in range(halves) if h not in line_first] + list(line_first):
                 wanted = gather(m, h)
@@ -653,9 +705,13 @@
             for way, peer in enumerate(peers, 1):
                 norm_copy(way, peer).wait_send()
 
+        def say_ready(m):
+            pl.semaphore_signal(
+                ready_sem.at[m], inc=1, device_id=(partner, section), device_id_type=MESH
+            )
+
+        say_ready(0)
         start_norms()
-        pl.semaphore_signal(ready_sem, inc=1, device_id=(partner, section), device_id_type=MESH)
-        pl.semaphore_wait(ready_sem, 1)
         total_units = len(parts) * units
 
         def of_unit(t, act):
@@ -663,7 +719,7 @@
 
                 @pl.when(t // units == m)
                 def _():
-                    act(m, level_of(lax.rem(t, units)))
+                    act(m, level_of(lax.rem(t, units)), t)
 
         def turn(t, carry):
             @pl.when(t < total_units)
@@ -673,18 +729,39 @@
             @pl.when(t == 0)
             def _():
                 spread_norms()
+                if len(parts) > 1:
+                    gradient_rows_left()
+                    say_ready(1)
+
+            if len(parts) > 1:
+
+                @pl.when(t == total_units + late - 1)
+                def _():
+                    last_unit(0)
 
             @pl.when(t >= late)
             def _():
-                of_unit(t - late, pass_unit)
+                of_unit(t - late, pass_line if line_first else pass_pair)
 
             return carry
 
         lax.fori_loop(0, total_units, turn, 0)
         send_output()
         lax.fori_loop(total_units, total_units + late, turn, 0)
-        for m in range(len(parts)):
-            last_unit(m)
+        if line_first:
+            pl.semaphore_wait(ready_sem.at[0], 1)
+            def start(j, carry):
+                send_pair(0, level_of(j), range(halves))
+                return carry
+
+            def end(j, carry):
+                pass_pair(0, level_of(j), j)
+                return carry
+
+            lax.fori_loop(0, units, start, 0)
+            last_line(0)
+            lax.fori_loop(0, units, end, 0)
+        last_unit(len(parts) - 1)
         finish_norms()
 
         def sent(k, carry):
@@ -710,59 +787,91 @@
 
     @pl.when(is_attention)
     def _():
-        if levels:
-            d_context[...] = jnp.zeros_like(d_context)
-            zeros = pltpu.make_async_copy(
-                d_context.at[:, pl.ds(0, hidden // (2 * levels))], down_out.at[0], load_sem.at[1]
-            )
-            zeros.start()
-            zeros.wait()
-        load_weight.wait()
         for which in range(3):
             columns = slice(which * width, (which + 1) * width)
+            load_weight(which).wait()
             down[:, columns] = weight[:, columns].T
+        for part in range(3, units):
+            load_weight(part).wait()
+        meet()
         ticks(
             lambda i: attend_forward(i, gain, shift, refs),
             lambda i: attend_backward(i, gain, refs),
         )
 
-        def first(k):
+        def first(k, some):
             columns = aligned(k, width)
 
             @pl.when(k < units - 1)
             def _():
-                weight[:, columns] = dot_tn(rows_in[...], keep[:, columns]).astype(bf16)
+                weight[some, columns] = dot_tn(rows_in[:, some], keep[:, columns]).astype(bf16)
 
             @pl.when(k == units - 1)
             def _():
-                weight[:, columns] = dot_tn(keep[:, columns], grad[...]).astype(bf16)
+                context = keep[:, 3 * width + some.start : 3 * width + some.stop]
+                weight[some, columns] = dot_tn(context, grad[...]).astype(bf16)
 
         weight_gradients(((first, weight, normal, first_out),), 1, (0,))
 
     @pl.when(is_feed)
     def _():
-        load_weight.wait()
+        for part in range(units):
+            load_weight(part).wait()
         load_down.wait()
+        meet()
         ticks(
             lambda i: feed_forward(aligned(i, length), gain, shift, refs),
             lambda i: feed_backward(aligned(i, length), gain, refs),
         )
 
-        gradient_rows_left()
-
-        def first(k):
+        def first(k, some):
             columns = aligned(k, width)
-            weight[:, columns] = dot_tn(rows_in[...], wide[:, columns]).astype(bf16)
-
-        def second(k):
+            weight[some, columns] = dot_tn(rows_in[:, some], wide[:, columns]).astype(bf16)
+
+        def second(k, some):
             columns = aligned(k, width)
-            down[:, columns] = dot_tn(grad[...], keep[:, columns]).astype(bf16)
+            down[some, columns] = dot_tn(grad[:, some], keep[:, columns]).astype(bf16)
 
         weight_gradients(
-            ((first, weight, normal, first_out), (second, down, d_in, down_out)), 2
+            ((first, weight, normal, first_out), (second, down, d_in, down_out)), 3
         )
 
     drain()
+
+
+def hand_over(*refs):
+    sources, norms, targets, (gain_out, shift_out) = refs[:4], refs[4], refs[5:9], refs[9:11]
+    held, sems = refs[11:15], refs[15]
+    has_down = lax.rem(lax.axis_index("section"), 2) == 1
+    fetch = [pltpu.make_async_copy(sources[i], held[i], sems.at[0, i]) for i in range(4)]
+    store = [pltpu.make_async_copy(held[i], targets[i], sems.at[1, i]) for i in range(4)]
+    for i in range(3):
+        fetch[i].start()
+
+    @pl.when(has_down)
+    def _():
+        fetch[3].start()
+
+    @pl.when(jnp.logical_not(has_down))
+    def _():
+        held[3][...] = jnp.zeros_like(held[3])
+        store[3].start()
+
+    width, own = norms.shape[1], gain_out.shape[1]
+    turned = pltpu.roll(norms[...], lax.rem(width - lax.axis_index("dp") * own, width), 1)
+    gain_out[...] = turned[0:1, :own]
+    shift_out[...] = turned[1:2, :own]
+    for i in range(3):
+        fetch[i].wait()
+        store[i].start()
+
+    @pl.when(has_down)
+    def _():
+        fetch[3].wait()
+        store[3].start()
+
+    for i in range(4):
+        store[i].wait()
 
 
 def on_device(tokens, cotangent, segment_ids, first_weight, down_weight, ln_gain, ln_shift):
@@ -796,9 +905,11 @@
         pltpu.VMEM((width, hidden), bf16),
         pltpu.VMEM((width, hidden), bf16),
         pltpu.VMEM((2, 8, width), f32),
-        pltpu.VMEM((width, max(length, columns_out if levels else 0)), f32),
+        pltpu.VMEM((width, length), f32),
         pltpu.VMEM((batches * 16, length), f32),
-        dma((2,)),
+        pltpu.VMEM((batches, length), jnp.int32),
+        pltpu.VMEM((2, 1, width), f32),
+        dma((units + 4,)),
         dma((batches,)),
         dma((batches,)),
         dma((batches,)),
@@ -810,22 +921,23 @@
     ]
     if levels:
         scratch += [
+            pltpu.VMEM((width, columns_out), f32),
             pltpu.VMEM((2, levels + 1, width, columns_out), bf16),
             pltpu.VMEM((levels, 8, width), f32),
             pltpu.VMEM((2, 8, width), f32),
-            pltpu.SemaphoreType.REGULAR,
-            dma((2, 2, levels, 2)),
-            dma((2, 2, levels + 1, 2)),
+            pltpu.SemaphoreType.REGULAR((2,)),
+            dma((2, 2, levels, HALVES)),
+            dma((2, 2, levels + 1, HALVES)),
             dma((2, levels)),
         ]
-    layer_rows, input_rows, first_sum, down_sum, norm_sum = pl.pallas_call(
+    results = pl.pallas_call(
         functools.partial(pipeline, sections, levels),
         out_shape=(
             jax.ShapeDtypeStruct((count // sections, width), bf16),
             jax.ShapeDtypeStruct((count // sections, width), bf16),
             *sums,
         ),
-        in_specs=[any_space, any_space, vmem, any_space, any_space, vmem, vmem],
+        in_specs=[any_space] * 7,
         out_specs=(any_space, any_space, any_space, any_space, vmem),
         scratch_shapes=scratch,
         compiler_params=pltpu.CompilerParams(
@@ -833,16 +945,22 @@
         ),
     )(tokens, cotangent, segment_ids, first_weight, down_weight, ln_gain, ln_shift)
     if levels:
-        own = width // groups
-        norm_sum = lax.dynamic_slice_in_dim(norm_sum, lax.axis_index("dp") * own, own, 1)
-    else:
-        has_down = lax.rem(lax.axis_index("section"), 2) == 1
-        down_sum = jnp.where(has_down, down_sum, jnp.zeros_like(down_sum))
-        first_sum, down_sum, norm_sum = (
-            lax.psum_scatter(value, "dp", scatter_dimension=1, tiled=True)
-            for value in (first_sum, down_sum, norm_sum)
-        )
-        first_sum, down_sum = first_sum.astype(f32)[None], down_sum.astype(f32)[None]
+        own = jax.ShapeDtypeStruct((1, width // groups), f32)
+        return pl.pallas_call(
+            hand_over,
+            out_shape=tuple(jax.ShapeDtypeStruct(r.shape, r.dtype) for r in results[:4]) + (own, own),
+            in_specs=[any_space] * 4 + [vmem],
+            out_specs=(any_space,) * 4 + (vmem,) * 2,
+            scratch_shapes=[pltpu.VMEM(r.shape, r.dtype) for r in results[:4]] + [dma((2, 4))],
+        )(*results)
+    layer_rows, input_rows, first_sum, down_sum, norm_sum = results
+    has_down = lax.rem(lax.axis_index("section"), 2) == 1
+    down_sum = jnp.where(has_down, down_sum, jnp.zeros_like(down_sum))
+    first_sum, down_sum, norm_sum = (
+        lax.psum_scatter(value, "dp", scatter_dimension=1, tiled=True)
+        for value in (first_sum, down_sum, norm_sum)
+    )
+    first_sum, down_sum = first_sum.astype(f32)[None], down_sum.astype(f32)[None]
     return (layer_rows, input_rows, first_sum, down_sum, norm_sum[0:1], norm_sum[1:2])
 
 

time: 184 us -> 174 us (0.946)
  local copies, waits for them, and re-layouts: 7.61 us -> 0 us
  Pallas kernels: 176 us -> 173 us
    pallas_call x1, Pallas kernels: 176 us -> 168 us  [on_device(): pl.pallas_call(functools.partial(pipeline, sections, levels), out_shape=(...]
    unnamed x8 -> x0, local copies, waits for them, and re-layouts: 6.16 us -> none
    pallas_call x0 -> x1, Pallas kernels: none -> 4.53 us  [on_device(): pl.pallas_call(hand_over, out_shape=tuple((jax.ShapeDtypeStruct(r.shape,...]
where the time goes in v3:
time: 174 us; the launch traced here: 173 us
  Pallas kernels  173 us (99%)
    pallas_call x1, Pallas kernels, on_device(): pl.pallas_call(functools.partial(pipeline, sections, levels), out_shape=(...  168 us
    pallas_call x1, Pallas kernels, on_device(): pl.pallas_call(hand_over, out_shape=tuple((jax.ShapeDtypeStruct(r.shape,...  4.53 us

profile of v3, /device:TPU:1, one launch (start us, length us, event | category | flops | bytes accessed | tf_op | source)
XLA Modules:
  0.0 173.4 jit_solution(2987043294111481360)
XLA Ops:
  0.6 168.0 %shard_map.118 = (bf16[512,768]{1,0:T(8,128)(2,1)}, bf16[512,768]{1,0:T(8,128)(2,1)}, f32[1,768,384]{2,1,0:T(8,128)}, f32[1,768,384]{2,1,0:T(8,128)}, f32[8,768]{1,0:T(8,128)}) custom-call(bf16[2048,768]{1,0:T(8,128)(2,1)} %tokens.1, bf16[2048,768]{1,0:T(8,128)(2,1)} %cotangent.1, s32[8,256]{1,0:T(8,128)} %segments_in.1, bf16[1,768,3072]{2,1,0:T(8,128)(2,1)} %weight_in.1, ...), custom_call_target="tpu_custom_call" | custom-call | tf_op jit(solution)/shard_map/pallas_call | solution.py:933
  168.6 4.5 %shard_map.119 = (bf16[512,768]{1,0:T(8,128)(2,1)}, bf16[512,768]{1,0:T(8,128)(2,1)}, f32[1,768,384]{2,1,0:T(8,128)}, f32[1,768,384]{2,1,0:T(8,128)}, f32[1,96]{1,0:T(1,128)}, /*index=5*/f32[1,96]{1,0:T(1,128)}) custom-call(bf16[512,768]{1,0:T(8,128)(2,1)} %get-tuple-element.11.refs_0_, bf16[512,768]{1,0:T(8,128)(2,1)} %get-tuple-element.12.refs_1_, ...), custom_call_target="tpu_custom_call" | custom-call | tf_op jit(solution)/shard_map/pallas_call | solution.py:949

commit v4 on v3

--- a/solution.py
+++ b/solution.py
@@ -335,6 +335,11 @@
     load_weight(0).start()
     for copy in small:
         copy.start()
+
+    @pl.when(section == 0)
+    def _():
+        load_rows(tokens, rows_in, 0).start()
+
     for part in range(1, units):
         load_weight(part).start()
 
@@ -344,7 +349,7 @@
 
     @pl.when(section == 0)
     def _():
-        for i in range(batches):
+        for i in range(1, batches):
             load_rows(tokens, rows_in, i).start()
 
     @pl.when(section == final)
@@ -534,6 +539,8 @@
 
             lax.fori_loop(0, units, unit, 0)
         send_output()
+        if len(parts) > 1:
+            gradient_rows_left()
         norm_out[...] = jnp.sum(norm_sums[...], axis=1)
         for m, (make, source, _, target) in enumerate(parts):
             for k in range(units):

time: 174 us -> 174 us (level)
  no operation moved by 1% of the time
where the time goes in v4:
time: 174 us; the launch traced here: 173 us
  Pallas kernels  173 us (99%)
    pallas_call x1, Pallas kernels, on_device(): pl.pallas_call(functools.partial(pipeline, sections, levels), out_shape=(...  168 us
    pallas_call x1, Pallas kernels, on_device(): pl.pallas_call(hand_over, out_shape=tuple((jax.ShapeDtypeStruct(r.shape,...  4.53 us

profile of v4, /device:TPU:1, one launch (start us, length us, event | category | flops | bytes accessed | tf_op | source)
XLA Modules:
  0.0 173.4 jit_solution(2987043294111481360)
XLA Ops:
  0.6 168.0 %shard_map.118 = (bf16[512,768]{1,0:T(8,128)(2,1)}, bf16[512,768]{1,0:T(8,128)(2,1)}, f32[1,768,384]{2,1,0:T(8,128)}, f32[1,768,384]{2,1,0:T(8,128)}, f32[8,768]{1,0:T(8,128)}) custom-call(bf16[2048,768]{1,0:T(8,128)(2,1)} %tokens.1, bf16[2048,768]{1,0:T(8,128)(2,1)} %cotangent.1, s32[8,256]{1,0:T(8,128)} %segments_in.1, bf16[1,768,3072]{2,1,0:T(8,128)(2,1)} %weight_in.1, ...), custom_call_target="tpu_custom_call" | custom-call | tf_op jit(solution)/shard_map/pallas_call | solution.py:940
  168.6 4.5 %shard_map.119 = (bf16[512,768]{1,0:T(8,128)(2,1)}, bf16[512,768]{1,0:T(8,128)(2,1)}, f32[1,768,384]{2,1,0:T(8,128)}, f32[1,768,384]{2,1,0:T(8,128)}, f32[1,96]{1,0:T(1,128)}, /*index=5*/f32[1,96]{1,0:T(1,128)}) custom-call(bf16[512,768]{1,0:T(8,128)(2,1)} %get-tuple-element.11.refs_0_, bf16[512,768]{1,0:T(8,128)(2,1)} %get-tuple-element.12.refs_1_, ...), custom_call_target="tpu_custom_call" | custom-call | tf_op jit(solution)/shard_map/pallas_call | solution.py:956
